TPU v7x, 512 devices: a whole 4x4x16 slice. The times are simulated.
512 devices in a mesh: dp: 128 (over y, z, core), replica: 4 (over x).
Axes of the slice: x: 4, y: 4, z: 16, core: 2. Of those that a mesh axis runs over, the one named last changes fastest.
Arguments:
- grad_local: float32 [4, 128, 4096, 128], P('replica', 'dp'), may hold values from -384 to 384
- first_moment: float32 [4, 4096, 128], P('replica', 'dp'), as said below
- second_moment: float32 [4, 4096, 128], P('replica', 'dp'), as said below
- master_weight: float32 [4, 4096, 128], P('replica', 'dp'), as said below
- lost_rows: int32 [4, 128], replicated, may hold values from 0 to 1, as said below
- source: int32 [4096], replicated, may hold values from 0 to 3, as said below
- new_owner: int32 [4096], replicated, may hold values from 0 to 127, as said below
- new_slot: int32 [4096], replicated, may hold values from 0 to 31
Outputs:
- fresh_first_moment: float32 [4096, 128], P('dp')
- new_second_moment: float32 [4096, 128], P('dp')
- new_weight: float32 [4096, 128], P('dp')
Inputs may be any that keep to these rules, and one draw needn't show every extreme that they name: `lost_rows`: every dp index survives in at least one replica group. source[b] names a replica group whose rank at dp index b // 32 is not lost; copies held by lost ranks are unrelated values. `new_owner`: together with new_slot a bijection onto owner and slot pairs: every dp index receives 32 blocks at distinct slots. Every old owner keeps 4 of its own blocks and hands at most 1 block to any one other dp index; that bound is reached in every draw. `first_moment`: equal on all replica groups except at lost ranks. `second_moment`: equal on all replica groups except at lost ranks; positive where not lost. `master_weight`: equal on all replica groups except at lost ranks.
All inputs are finite; a program needn't handle non-finite values.
Results may differ from a plain program's by a relative error of at most 0.000071.
Values sent between devices are 32-bit elements; how exact they have to be, the bound alone decides.
A program may use at most 64 MiB of HBM per device.

v0:
```python
import jax
import jax.numpy as jnp
from jax import lax
from jax.sharding import PartitionSpec as P

BETA_ONE = 0.9
BETA_TWO = 0.95
BIAS_FIRST = 1.0 - 0.9**10
BIAS_SECOND = 1.0 - 0.95**10
EPSILON = 1e-08
LEARN_RATE = 0.1
DECAY_RATE = 0.1


def adamw_update(moment_one, moment_two, weight, gradient_rows):
    first = BETA_ONE * moment_one + (1.0 - BETA_ONE) * gradient_rows
    second = BETA_TWO * moment_two + (1.0 - BETA_TWO) * gradient_rows * gradient_rows
    update = first / BIAS_FIRST / (jnp.sqrt(second / BIAS_SECOND) + EPSILON)
    return (first, second, weight - LEARN_RATE * (update + DECAY_RATE * weight))


def gradient_total(resident_term):
    dp_partial = lax.psum_scatter(resident_term, "dp", scatter_dimension=0, tiled=True)
    return lax.psum(dp_partial, "replica")


def on_device(
    grad_local, first_moment, second_moment, master_weight, lost_rows, source, new_owner, new_slot
):
    replica_at = lax.axis_index("replica")
    dp_at = lax.axis_index("dp")
    dp_count = lax.axis_size("dp")
    blocks = first_moment.shape[1]
    lane_count = first_moment.shape[2]
    all_blocks = new_owner.shape[0]
    living_flags = (1 - lost_rows).astype(jnp.float32)
    living_replicas = jnp.sum(living_flags)
    resident_term = grad_local[0, 0] * living_flags[replica_at, dp_at]
    placed = new_owner * blocks + new_slot
    fresh_ordering = (
        jnp.zeros((all_blocks,), jnp.int32).at[placed].set(jnp.arange(all_blocks, dtype=jnp.int32))
    )
    first_block = dp_at * blocks
    own_source = lax.dynamic_slice_in_dim(source, first_block, blocks)
    stacked = jnp.concatenate([first_moment[0], second_moment[0], master_weight[0]], axis=1)
    chosen = jnp.where((own_source == replica_at)[:, None], stacked, 0.0)
    repaired = lax.psum(chosen, "replica")
    gradient_rows = gradient_total(resident_term[fresh_ordering]) / living_replicas
    own_dest = lax.dynamic_slice_in_dim(new_owner, first_block, blocks)
    moving = own_dest != dp_at
    positions = jnp.arange(blocks, dtype=jnp.int32)
    earlier = positions[:, None] > positions[None, :]
    same_dest = (own_dest[:, None] == own_dest[None, :]) & earlier
    send_rank = jnp.sum(same_dest.astype(jnp.int32), axis=1)
    capacity = (blocks - blocks // 8 + dp_count - 2) // (dp_count - 1)
    slot_count = dp_count * capacity
    send_at = jnp.where(moving, own_dest * capacity + send_rank, slot_count)
    outgoing = (
        jnp.zeros((slot_count, repaired.shape[1]), jnp.float32)
        .at[send_at]
        .set(repaired, mode="drop")
    )
    outgoing = outgoing.reshape(dp_count, capacity, repaired.shape[1])
    arrived = lax.all_to_all(outgoing, "dp", split_axis=0, concat_axis=0, tiled=True)
    arrived = arrived.reshape(slot_count, repaired.shape[1])
    my_blocks = lax.dynamic_slice_in_dim(fresh_ordering, first_block, blocks)
    from_owner = my_blocks // blocks
    from_resident = my_blocks % blocks
    headed_here = (new_owner == dp_at).astype(jnp.int32).reshape(dp_count, blocks)
    before = jnp.cumsum(headed_here, axis=1) - headed_here
    arrive_rank = before[from_owner, from_resident]
    staying = from_owner == dp_at
    from_arrived = arrived[jnp.minimum(from_owner * capacity + arrive_rank, slot_count - 1)]
    from_home = repaired[from_resident]
    gathered = jnp.where(staying[:, None], from_home, from_arrived)
    moment_in = gathered[:, :lane_count]
    second_in = gathered[:, lane_count : 2 * lane_count]
    weight_in = gathered[:, 2 * lane_count : 3 * lane_count]
    return adamw_update(moment_in, second_in, weight_in, gradient_rows)


def solution(mesh):
    return jax.shard_map(
        on_device,
        mesh=mesh,
        in_specs=(
            P("replica", "dp", None, None),
            P("replica", "dp", None),
            P("replica", "dp", None),
            P("replica", "dp", None),
            P(),
            P(),
            P(),
            P(),
        ),
        out_specs=(P("dp", None), P("dp", None), P("dp", None)),
        check_vma=False,
    )
```

profile of v0, /device:TPU:24, one launch (start us, length us, event | category | flops | bytes accessed | tf_op | source)
XLA Modules:
  0.0 409.8 jit_solution(13223732380928114989)
XLA Ops:
  7.2 0.0 reduce-scatter.2.cloned.1.call-start
  7.2 0.7 subtract_convert_fusion
  7.9 0.7 compare_select_fusion.1
  8.7 15.5 %scatter_custom_fusion = s32[4096]{0:T(1024)S(1)} fusion(s32[4096]{0:T(1024)S(1)} %compare_select_fusion.1, s32[4096]{0:T(1024)S(1)} %iota.10, s32[]{:T(128)} %constant.23.clone.1), kind=kCustom, calls=%fused_computation.26 | custom fusion | bytes 16388 | tf_op jit(solution)/shard_map/scatter | solution.py:41
  24.2 0.6 dynamic_slice.15
  24.8 2.4 multiply_bitcast_fusion
  27.2 14.2 %gather_fusion.3 = f32[4096,128]{1,0:T(8,128)} fusion(f32[4096,128]{1,0:T(8,128)S(1)} %multiply_bitcast_fusion, s32[4096]{0:T(1024)S(1)} %fusion.3), kind=kCustom, calls=%fused_computation.3 | custom fusion | bytes 4210688 | tf_op jit(solution)/shard_map/gather | solution.py:48
  41.3 0.0 copy-start
  41.3 0.0 copy-start.2
  41.3 0.0 copy-start.3
  41.3 0.0 copy-start.4
  41.3 0.0 copy-start.5
  41.3 0.0 reduce-scatter.2.cloned.1.call-update
  41.4 0.0 all-reduce.3.cloned.1.call-start
  41.4 0.6 copy-done
  42.0 0.1 dynamic_slice.14
  42.1 0.1 reshape.29
  42.2 0.1 copy.15
  42.3 0.1 reduce_window_sum.11
  42.3 0.8 dynamic-slice_compare_fusion
  43.1 0.2 convert_reduce_fusion
  43.3 0.1 compare_select_fusion.4
  43.4 0.0 copy-done.2
  43.4 0.0 copy-done.3
  43.4 0.0 copy-done.4
  43.4 0.7 maximum_select_fusion
  44.1 262.3 %reduce-scatter.2.cloned.1.call-done = f32[32,128]{1,0:T(8,128)} async-done(((f32[4096,128]{1,0:T(8,128)}), f32[32,128]{1,0:T(8,128)}) %reduce-scatter.2.cloned.1.call-update) | async-done | bytes 16400 | tf_op jit(solution)/shard_map/reduce_scatter | solution.py:23
  306.4 0.0 all-reduce.3.cloned.1.call-update
  306.4 0.1 broadcast_compare_fusion
  306.5 56.8 %all-reduce.3.cloned.1.call-done = (f32[32,384]{1,0:T(8,128)}, f32[32,128]{1,0:T(8,128)}) async-done(((f32[32,384]{1,0:T(8,128)}, f32[32,128]{1,0:T(8,128)}), (f32[32,384]{1,0:T(8,128)}, f32[32,128]{1,0:T(8,128)})) %all-reduce.3.cloned.1.call-update) | async-done | bytes 65552 | tf_op jit(solution)/shard_map/psum | solution.py:47
  363.4 0.0 copy-start.1
  363.4 1.0 scatter_custom_fusion.1
  364.4 0.8 reshape.24
  365.2 17.0 %all-to-all-start = ((f32[128,1,384]{2,1,0:T(1,128)}), f32[128,1,384]{2,1,0:T(1,128)S(1)}, u32[]{:S(2)}, u32[]{:S(2)}) async-start(f32[128,1,384]{2,1,0:T(1,128)} %reshape.24), calls=%async_computation | async-start | bytes 393216 | tf_op jit(solution)/shard_map/all_to_all | solution.py:64
  382.2 0.7 gather_fusion.1
  382.9 0.0 copy-done.5
  382.9 0.6 fusion.11
  383.6 1.4 gather_fusion
  385.0 15.9 %all-to-all-done = f32[128,1,384]{2,1,0:T(1,128)S(1)} async-done(((f32[128,1,384]{2,1,0:T(1,128)}), f32[128,1,384]{2,1,0:T(1,128)S(1)}, u32[]{:S(2)}, u32[]{:S(2)}) %all-to-all-start) | async-done | bytes 196640 | tf_op jit(solution)/shard_map/all_to_all | solution.py:64
  401.0 0.6 gather_fusion.2
  401.6 0.1 broadcast_select_fusion
  401.7 0.0 copy-done.1
  401.7 1.3 multiply_subtract_fusion
  (9 shorter events, 0.1 us)
Async XLA Ops:
  7.2 299.2 %reduce-scatter.2.cloned.1.call-start = ((), (), s32[]{:S(2)}) async-start(), calls=%async_computation.2 | async-start | bytes 2113536 | tf_op jit(solution)/shard_map/reduce_scatter | solution.py:23
  41.3 0.7 copy-start
  41.3 2.0 copy-start.2
  41.3 2.0 copy-start.3
  41.3 2.0 copy-start.4
  41.3 341.6 %copy-start.5 = (s32[4,128]{1,0:T(4,128)S(1)}, s32[4,128]{1,0:T(4,128)}, u32[]{:S(2)}) copy-start(s32[4,128]{1,0:T(4,128)} %param.12) | copy-start | bytes 6148
  41.4 322.0 %all-reduce.3.cloned.1.call-start = ((), (), s32[]{:S(2)}) async-start(), calls=%async_computation.3 | async-start | bytes 131072 | tf_op jit(solution)/shard_map/psum | solution.py:47
  363.4 38.3 %copy-start.1 = (f32[32,128]{1,0:T(8,128)S(1)}, f32[32,128]{1,0:T(8,128)}, u32[]{:S(2)}) copy-start(f32[32,128]{1,0:T(8,128)} %get-tuple-element.4) | copy-start | bytes 49156
  365.2 35.8 %all-to-all-start = ((f32[128,1,384]{2,1,0:T(1,128)}), f32[128,1,384]{2,1,0:T(1,128)S(1)}, u32[]{:S(2)}, u32[]{:S(2)}) async-start(f32[128,1,384]{2,1,0:T(1,128)} %reshape.24), calls=%async_computation | async-start | bytes 393216 | tf_op jit(solution)/shard_map/all_to_all | solution.py:64
Sparse Core Ops, SparseCore 0:
  41.5 264.8 reduce-scatter.1
  308.8 54.4 all-reduce.2
where the time goes:
time: 412 us; the launch traced here: 410 us
  waiting for transfers between devices  335 us (81%)
  local copies, waits for them, and re-layouts  35.7 us (9%)
  starting transfers between devices  17.1 us (4%)
  between operations  14.1 us (3%)
  other arithmetic  7.7 us (2%)
    reduce_scatter x1, waiting for transfers between devices, gradient_total(): lax.psum_scatter(resident_term, 'dp', scatter_dimension=0, tiled=True)  262 us
    psum x1, waiting for transfers between devices, on_device(): repaired = lax.psum(chosen, 'replica')  56.8 us
    all_to_all x1, starting transfers between devices, on_device(): lax.all_to_all(outgoing, 'dp', split_axis=0, concat_axis=0, tiled=True)  17 us
    all_to_all x1, waiting for transfers between devices, on_device(): lax.all_to_all(outgoing, 'dp', split_axis=0, concat_axis=0, tiled=True)  15.9 us
    scatter x1, local copies, waits for them, and re-layouts, on_device(): jnp.zeros((all_blocks,), jnp.int32).at[placed]  15.5 us
    gather x1, local copies, waits for them, and re-layouts, on_device(): resident_term[fresh_ordering]  14.2 us
  transfers between devices with their start and end apart: 3, of which 3 were waited for; matrix products, arithmetic and copies ran while one was open for 1% of the time, Pallas kernels for 0%

commit v1 on v0

v1 whole, which is shorter than its diff:
```python
import functools
import math

import jax
import jax.numpy as jnp
from jax import lax
from jax.experimental import pallas as pl
from jax.experimental.pallas import tpu as pltpu
from jax.sharding import PartitionSpec as P

BETA_ONE = 0.9
BETA_TWO = 0.95
BIAS_FIRST = 1.0 - 0.9**10
BIAS_SECOND = 1.0 - 0.95**10
EPSILON = 1e-08
LEARN_RATE = 0.1
DECAY_RATE = 0.1

NX = 4
NY = 4
NZ = 16
JR = 8
LANES = 128
UNROLL = 32

MESH = pl.DeviceIdType.MESH
F32 = jnp.float32
BF16 = jnp.bfloat16
I32 = jnp.int32


def log2(n):
    return int(math.log2(n))


def iota(shape, dim):
    return lax.broadcasted_iota(I32, shape, dim)


def three_parts(value):
    one = value.astype(BF16)
    rest = value - one.astype(F32)
    two = rest.astype(BF16)
    three = (rest - two.astype(F32)).astype(BF16)
    return one, two, three


def pick(onehot, parts):
    total = jnp.dot(onehot, parts[2], preferred_element_type=F32)
    total = total + jnp.dot(onehot, parts[1], preferred_element_type=F32)
    return total + jnp.dot(onehot, parts[0], preferred_element_type=F32)


def prepare(owner_ref, slot_ref, source_ref, m_ref, v_ref, w_ref, lost_ref,
            order_ref, out_ref, wsel_ref, stay_ref, aux_ref, held):
    blk = NX * JR
    segs = LANES // blk
    rows = owner_ref.shape[0]
    zh = NZ // 2
    x = lax.axis_index("replica")
    dp = lax.axis_index("dp")
    y = dp // (2 * NZ)
    c = dp % 2
    partner = dp + 1 - 2 * c

    living = (1 - lost_ref[...]).astype(F32)
    at_row = iota(living.shape, 0)
    at_col = iota(living.shape, 1)
    mine = jnp.sum(jnp.where((at_row == x) & (at_col == dp), living, 0.0))
    other = jnp.sum(jnp.where((at_row == x) & (at_col == partner), living, 0.0))
    aux_ref[0:8, :] = jnp.full((8, LANES), mine, F32)
    aux_ref[8:16, :] = jnp.full((8, LANES), other, F32)
    aux_ref[16:24, :] = jnp.full((8, LANES), jnp.sum(living), F32)

    owner = owner_ref[...]
    slot = slot_ref[...]
    oy = owner >> log2(2 * NZ)
    oz = (owner >> 1) & (NZ - 1)
    oc = owner & 1
    ox = slot >> log2(JR)
    oj = slot & (JR - 1)
    half = oz >> log2(zh)
    zl = oz & (zh - 1)
    first = jnp.where(half == 0, ox, oy)
    second = jnp.where(half == 0, oy, ox)
    pos = ((((oc * 2 + half) * NX + first) * NY + second) * zh + zl) * JR + oj
    pos_row = pos >> 7
    pos_col = pos & 127
    row_pad = max(rows, 8)
    sub_row = iota((row_pad, LANES), 0)
    sub_col = iota((LANES, LANES), 0)
    lane = iota((1, LANES), 1)
    left, right = [], []
    for r in range(rows):
        hit = sub_row == pos_row[r:r + 1, :]
        high = (2 * r + (lane >> 6)).astype(F32)
        low = (lane & 63).astype(F32)
        left.append(jnp.concatenate(
            [jnp.where(hit, high, 0.0), jnp.where(hit, low, 0.0)], axis=0).astype(BF16))
        right.append(jnp.where(sub_col == pos_col[r:r + 1, :], 1.0, 0.0).astype(BF16))
    both = lax.dot_general(
        jnp.concatenate(left, axis=1), jnp.concatenate(right, axis=1),
        (((1,), (1,)), ((), ())), preferred_element_type=F32)
    order = both[:row_pad] * 64.0 + both[row_pad:]
    order_ref[...] = order[:rows].astype(I32)

    seg = dp % segs
    held[...] = jnp.zeros_like(held)
    at = pl.ds(pl.multiple_of(seg * blk, 8), blk)
    keep = jnp.full((blk, LANES), mine, F32) > 0.5
    held[at, 0:128] = jnp.where(keep, m_ref[...], 0.0)
    held[at, 128:256] = jnp.where(keep, v_ref[...], 0.0)
    held[at, 256:384] = jnp.where(keep, w_ref[...], 0.0)
    parts = three_parts(held[...])
    own_row = dp // segs
    owner_row = owner_ref[pl.ds(own_row, 1), :]
    slot_row = slot_ref[pl.ds(own_row, 1), :]
    source_row = source_ref[pl.ds(own_row, 1), :]
    here = ((lane >> log2(blk)) == seg) & (source_row == x)

    leaving = jnp.where(here & (owner_row != dp), owner_row, -2)
    total_rows = NY * NZ * 8
    at_dest = iota((total_rows, LANES), 0)
    pair = at_dest >> 3
    sub = at_dest & 7
    result = None
    for k in range(3):
        dest = jnp.where(sub == k, 2 * pair, jnp.where(sub == 3 + k, 2 * pair + 1, -1))
        onehot = jnp.where(dest == leaving, 1.0, 0.0).astype(BF16)
        got = pick(onehot, [p[:, k * 128:(k + 1) * 128] for p in parts])
        result = got if result is None else result + got
    out_ref[...] = result

    staying = jnp.where(here & (owner_row == dp), slot_row, -1)
    onehot = jnp.where(iota((blk, LANES), 0) == staying, 1.0, 0.0).astype(BF16)
    got = pick(onehot, parts)
    for k in range(3):
        stay_ref[k * blk:(k + 1) * blk, :] = got[:, k * 128:(k + 1) * 128]

    group_rows = 2 * NZ * blk // LANES
    from_y = (x - y + NX) % NX
    at = pl.ds(pl.multiple_of(from_y * group_rows, group_rows), group_rows)
    block = (from_y * group_rows + iota((group_rows, LANES), 0)) * LANES + iota((group_rows, LANES), 1)
    coming = (owner_ref[at, :] == dp) & ((block >> log2(blk)) != dp)
    named = jnp.where(coming, slot_ref[at, :] + 1, 0).astype(F32)
    cols = 2 * NZ * 8
    def source_of(shape):
        col = iota(shape, 1)
        core = jnp.where(col >= NZ * 8, 1 - c, c)
        return ((col & (NZ * 8 - 1)) >> 3) * 2 + core
    spread = jnp.where(
        (iota((LANES, cols), 0) >> log2(blk)) == (source_of((LANES, cols)) & (segs - 1)), 1.0, 0.0)
    if group_rows < 8:
        named = jnp.concatenate([named, jnp.zeros((8 - group_rows, LANES), F32)], axis=0)
    table = jnp.dot(named.astype(BF16), spread.astype(BF16), preferred_element_type=F32)
    row_of = source_of((8, cols)) >> log2(segs)
    slots = jnp.sum(jnp.where(iota((8, cols), 0) == row_of, table, 0.0), axis=0, keepdims=True)
    at_row = iota((3 * blk, cols), 0)
    kind = at_row >> log2(blk)
    sub = iota((3 * blk, cols), 1) & 7
    wanted = ((at_row & (blk - 1)) + 1).astype(F32)
    wsel_ref[...] = jnp.where((slots == wanted) & (sub == 3 * c + kind), 1.0, 0.0)


def exchange(order, grad_hbm, out_ref, wsel_ref, stay_ref, aux_ref,
             first_ref, second_ref, weight_ref,
             grad, csend, crecv, own, rx0, rx1, t0, t1, ry0, ry1, u, rz, gfull,
             srecv, ssum, r1, r2, r3, pbuf, precv,
             grad_sem, csend_sem, crecv_sem, send_sem, recv_sem):
    blk = NX * JR
    zh = NZ // 2
    chunk = NY * zh * JR
    piece = zh * JR
    x = lax.axis_index("replica")
    dp = lax.axis_index("dp")
    y = dp // (2 * NZ)
    z = (dp // 2) % NZ
    c = dp % 2

    def device(dx=0, dy=0, dz=0, dc=0):
        to_y = (y + dy) % NY
        to_z = (z + dz) % NZ
        to_c = (c + dc) % 2
        return ((to_y * NZ + to_z) * 2 + to_c, (x + dx) % NX)

    load = pltpu.make_async_copy(grad_hbm, grad, grad_sem)
    load.start()

    barrier = pltpu.get_barrier_semaphore()
    peers = ([dict(dc=1)] + [dict(dx=k) for k in range(1, NX)]
             + [dict(dy=k) for k in range(1, NY)])
    for peer in peers:
        pl.semaphore_signal(barrier, inc=1, device_id=device(**peer), device_id_type=MESH)

    def greet(k, carry):
        pl.semaphore_signal(barrier, inc=1, device_id=device(dz=k), device_id_type=MESH)
        return carry

    lax.fori_loop(1, NZ, greet, 0)

    def send(src, dst, to, s_sem, r_sem):
        pltpu.make_async_remote_copy(
            src_ref=src, dst_ref=dst, send_sem=s_sem, recv_sem=r_sem,
            device_id=to, device_id_type=MESH).start()

    def await_bytes(ref, sem):
        pltpu.make_async_copy(ref, ref, sem).wait()

    def gather(dst, dst_base, base):
        def step(i, carry):
            at = base + i * UNROLL
            values = [grad[pl.ds(order[at + k], 1), :] for k in range(UNROLL)]
            tile = dst.at[pl.ds(pl.multiple_of(dst_base + i * UNROLL, UNROLL), UNROLL)]
            for k in range(UNROLL):
                tile[k:k + 1, :] = values[k]
            return carry
        lax.fori_loop(0, chunk // UNROLL, step, 0)

    chunks = []
    for k in [2, 1, 3, 0] if NX == 4 else [1, 0]:
        chunks.append((0, k, pl.multiple_of(((x + k) % NX) * chunk, chunk)))
        chunks.append((1, k, pl.multiple_of((NX + (y + k) % NY) * chunk, chunk)))

    load.wait()
    core_rows = 2 * NX * chunk
    for i, (h, k, base) in enumerate(chunks):
        gather(csend, base, (1 - c) * core_rows + base)
        if i == 0:
            pl.semaphore_wait(barrier, len(peers) + NZ - 1)
            for dx in range(1, NX):
                to_y = (x + dx - y + NX) % NX
                send(out_ref.at[pl.ds(pl.multiple_of(to_y * NZ * 8, NZ * 8), NZ * 8)],
                     srecv.at[dx - 1], device(dx=dx), send_sem.at[0], recv_sem.at[0])
        rows = pl.ds(base, chunk)
        send(csend.at[rows], crecv.at[rows], device(dc=1), csend_sem, crecv_sem.at[i])

    alive_mine = aux_ref[0:1, :]
    alive_other = aux_ref[8:9, :]
    partner_y = (x - y + NX) % NX
    for i, (h, k, base) in enumerate(chunks):
        gather(own, base, c * core_rows + base)
        rows = pl.ds(base, chunk)
        await_bytes(crecv.at[rows], crecv_sem.at[i])
        own[rows, :] = own[rows, :] * alive_mine + crecv[rows, :] * alive_other
        if k > 0:
            to = device(dx=k) if h == 0 else device(dy=k)
            send(own.at[rows], (rx0 if h == 0 else rx1).at[k - 1], to,
                 send_sem.at[1 + h], recv_sem.at[1 + h])
        if i == len(chunks) // 2:
            await_bytes(srecv, recv_sem.at[0])
            total = out_ref[pl.ds(pl.multiple_of(partner_y * NZ * 8, NZ * 8), NZ * 8), :]
            for dx in range(NX - 1):
                total = total + srecv[dx]
            ssum[...] = total
            r1[z] = ssum[pl.ds(pl.multiple_of(z * 8, 8), 8), :]

            def spread(kz, carry):
                to_z = (z + kz) % NZ
                send(ssum.at[pl.ds(pl.multiple_of(to_z * 8, 8), 8)], r1.at[z],
                     device(dz=kz), send_sem.at[3], recv_sem.at[3])
                return carry

            lax.fori_loop(1, NZ, spread, 0)

    own0 = pl.multiple_of(x * chunk, chunk)
    own1 = pl.multiple_of((NX + y) * chunk, chunk)
    await_bytes(rx0, recv_sem.at[1])
    total = own[pl.ds(own0, chunk), :]
    for k in range(NX - 1):
        total = total + rx0[k]
    t0[...] = total
    for k in range(1, NY):
        at = pl.ds(pl.multiple_of(((y + k) % NY) * piece, piece), piece)
        send(t0.at[at], ry0.at[k - 1], device(dy=k), send_sem.at[4], recv_sem.at[4])
    await_bytes(rx1, recv_sem.at[2])
    total = own[pl.ds(own1, chunk), :]
    for k in range(NY - 1):
        total = total + rx1[k]
    t1[...] = total
    for k in range(1, NX):
        at = pl.ds(pl.multiple_of(((x + k) % NX) * piece, piece), piece)
        send(t1.at[at], ry1.at[k - 1], device(dx=k), send_sem.at[5], recv_sem.at[5])

    await_bytes(r1.at[0:NZ - 1], recv_sem.at[3])
    partner = ((partner_y * NZ + z) * 2 + c, x)

    @pl.when(partner_y != y)
    def _():
        send(r1, r2, partner, send_sem.at[6], recv_sem.at[6])

    @pl.when(partner_y == y)
    def _():
        r2[...] = r1[...]

    await_bytes(ry0, recv_sem.at[4])
    total = t0[pl.ds(pl.multiple_of(y * piece, piece), piece), :]
    for k in range(NY - 1):
        total = total + ry0[k]
    u[0:piece, :] = total
    await_bytes(ry1, recv_sem.at[5])
    total = t1[pl.ds(pl.multiple_of(x * piece, piece), piece), :]
    for k in range(NX - 1):
        total = total + ry1[k]
    u[piece:2 * piece, :] = total

    def scatter(kz, carry):
        to_z = (z + kz) % NZ
        send(u.at[pl.ds(pl.multiple_of(to_z * JR, JR), JR)], rz.at[kz - 1],
             device(dz=kz), send_sem.at[7], recv_sem.at[7])
        return carry

    lax.fori_loop(1, NZ, scatter, 0)

    @pl.when(partner_y != y)
    def _():
        await_bytes(r2, recv_sem.at[6])

    send(r2, r3, device(dc=1), send_sem.at[8], recv_sem.at[8])
    half = NZ * 8
    near = three_parts(r2[...].reshape(half, LANES))
    total = stay_ref[...] + pick(wsel_ref[:, 0:half].astype(BF16), near)
    await_bytes(r3, recv_sem.at[8])
    far = three_parts(r3[...].reshape(half, LANES))
    pbuf[...] = total + pick(wsel_ref[:, half:2 * half].astype(BF16), far)
    for k in range(1, NX):
        send(pbuf, precv.at[k - 1], device(dx=k), send_sem.at[9], recv_sem.at[9])

    await_bytes(rz, recv_sem.at[7])
    total = u[pl.ds(pl.multiple_of(z * JR, JR), JR), :]
    for k in range(NZ - 1):
        total = total + rz[k]
    gfull[x] = total
    for k in range(1, NX):
        send(gfull.at[x], gfull.at[x], device(dx=k), send_sem.at[10], recv_sem.at[10])

    await_bytes(precv, recv_sem.at[9])
    state = pbuf[...]
    for k in range(NX - 1):
        state = state + precv[k]
    await_bytes(gfull.at[0:NX - 1], recv_sem.at[10])
    gradient = gfull[...].reshape(blk, LANES) / aux_ref[16:17, :]
    first = BETA_ONE * state[0:blk] + (1.0 - BETA_ONE) * gradient
    second = BETA_TWO * state[blk:2 * blk] + (1.0 - BETA_TWO) * gradient * gradient
    weight = state[2 * blk:3 * blk]
    update = first / BIAS_FIRST / (jnp.sqrt(second / BIAS_SECOND) + EPSILON)
    first_ref[...] = first
    second_ref[...] = second
    weight_ref[...] = weight - LEARN_RATE * (update + DECAY_RATE * weight)

    await_bytes(csend, csend_sem)
    for ref, n in ((srecv, 0), (rx0, 1), (rx1, 2), (r1.at[0:NZ - 1], 3), (ry0, 4), (ry1, 5),
                   (rz, 7), (r3, 8), (precv, 9), (gfull.at[0:NX - 1], 10)):
        await_bytes(ref, send_sem.at[n])

    @pl.when(partner_y != y)
    def _():
        await_bytes(r1, send_sem.at[6])


def on_device(grad_local, first_moment, second_moment, master_weight, lost_rows, source,
              new_owner, new_slot):
    blk = NX * JR
    nblk = new_owner.shape[0]
    rows = nblk // LANES
    half_z = NZ * 8
    vmem = pl.BlockSpec(memory_space=pltpu.VMEM)
    order, out, wsel, stay, aux = pl.pallas_call(
        prepare,
        out_shape=(
            jax.ShapeDtypeStruct((rows, LANES), I32),
            jax.ShapeDtypeStruct((NY * half_z, LANES), F32),
            jax.ShapeDtypeStruct((3 * blk, 2 * half_z), F32),
            jax.ShapeDtypeStruct((3 * blk, LANES), F32),
            jax.ShapeDtypeStruct((24, LANES), F32),
        ),
        in_specs=[vmem] * 7,
        out_specs=[vmem] * 5,
        scratch_shapes=[pltpu.VMEM((LANES, 3 * LANES), F32)],
        compiler_params=pltpu.CompilerParams(vmem_limit_bytes=24 * 2**20),
    )(new_owner.reshape(rows, LANES), new_slot.reshape(rows, LANES), source.reshape(rows, LANES),
      first_moment[0], second_moment[0], master_weight[0], lost_rows)

    zh = NZ // 2
    chunk = NY * zh * JR
    piece = zh * JR
    half_rows = 2 * NX * chunk

    def buf(*shape):
        return pltpu.VMEM(shape + (LANES,), F32)

    dma = pltpu.SemaphoreType.DMA
    result = jax.ShapeDtypeStruct((blk, LANES), F32)
    return pl.pallas_call(
        exchange,
        out_shape=(result,) * 3,
        in_specs=[pl.BlockSpec(memory_space=pltpu.SMEM), pl.BlockSpec(memory_space=pl.ANY)]
        + [vmem] * 4,
        out_specs=[vmem] * 3,
        scratch_shapes=[
            buf(nblk), buf(half_rows), buf(half_rows), buf(half_rows),
            buf(NX - 1, chunk), buf(NY - 1, chunk), buf(chunk), buf(chunk),
            buf(NY - 1, piece), buf(NX - 1, piece), buf(2 * piece),
            buf(NZ - 1, JR), buf(NX, JR),
            buf(NX - 1, half_z), buf(half_z), buf(NZ, 8), buf(NZ, 8), buf(NZ, 8),
            buf(3 * blk), buf(NX - 1, 3 * blk),
            dma, dma, dma((2 * NX,)), dma((11,)), dma((11,)),
        ],
        compiler_params=pltpu.CompilerParams(
            collective_id=0, has_side_effects=True, vmem_limit_bytes=32 * 2**20),
        cost_estimate=pl.CostEstimate(
            flops=nblk * LANES, bytes_accessed=nblk * LANES * 4, transcendentals=0),
    )(order.reshape(nblk), grad_local[0, 0], out, wsel, stay, aux)


def solution(mesh):
    return jax.shard_map(
        on_device,
        mesh=mesh,
        in_specs=(
            P("replica", "dp", None, None),
            P("replica", "dp", None),
            P("replica", "dp", None),
            P("replica", "dp", None),
            P(),
            P(),
            P(),
            P(),
        ),
        out_specs=(P("dp", None), P("dp", None), P("dp", None)),
        check_vma=False,
    )
```

time: 412 us -> 52.6 us (0.13)
  waiting for transfers between devices: 335 us -> 0 us
  Pallas kernels: 0 us -> 42.5 us
  local copies, waits for them, and re-layouts: 35.7 us -> 8.38 us
  starting transfers between devices: 17.1 us -> 0 us
  between operations: 14.1 us -> 0.67 us
  other arithmetic: 7.7 us -> 0 us
    reduce_scatter x1 -> x0, waiting for transfers between devices: 262 us -> none  [gradient_total(): lax.psum_scatter(resident_term, 'dp', scatter_dimension=0, tiled=True)]
    psum x1 -> x0, waiting for transfers between devices: 56.8 us -> none  [on_device(): repaired = lax.psum(chosen, 'replica')]
    pallas_call x0 -> x2, Pallas kernels: none -> 42.5 us  [the longest x1 41.5 us: on_device(): pl.pallas_call(exchange, out_shape=(result,) * 3, in_specs=[pl.BlockSpec(...]
    all_to_all x1 -> x0, starting transfers between devices: 17 us -> none  [on_device(): lax.all_to_all(outgoing, 'dp', split_axis=0, concat_axis=0, tiled=True)]
    gather x4 -> x0, local copies, waits for them, and re-layouts: 16.9 us -> none  [the longest x1 14.2 us: on_device(): resident_term[fresh_ordering]]
    scatter x2 -> x0, local copies, waits for them, and re-layouts: 16.5 us -> none  [the longest x1 15.5 us: on_device(): jnp.zeros((all_blocks,), jnp.int32).at[placed]]
    all_to_all x1 -> x0, waiting for transfers between devices: 15.9 us -> none  [on_device(): lax.all_to_all(outgoing, 'dp', split_axis=0, concat_axis=0, tiled=True)]
    unnamed x13 -> x19, local copies, waits for them, and re-layouts: 0.65 us -> 8.38 us
  transfers between devices with their start and end apart: 3 -> 0, of which waited for: 3 -> 0; matrix products, arithmetic and copies ran while one was open for 1% -> 0% of each run, Pallas kernels for 0% -> 0%
where the time goes in v1:
time: 52.6 us; the launch traced here: 51.6 us
  Pallas kernels  42.5 us (81%)
  local copies, waits for them, and re-layouts  8.38 us (16%)
  between operations  0.67 us (1%)
    pallas_call x1, Pallas kernels, on_device(): pl.pallas_call(exchange, out_shape=(result,) * 3, in_specs=[pl.BlockSpec(...  41.5 us
    unnamed x19, local copies, waits for them, and re-layouts  8.38 us

profile of v1, /device:TPU:24, one launch (start us, length us, event | category | flops | bytes accessed | tf_op | source)
XLA Modules:
  0.0 51.6 jit_solution(11385936362821691536)
XLA Ops:
  0.6 0.0 copy-start.1
  0.6 0.7 %copy-done.1 = s32[4096]{0:T(1024)S(1)} copy-done((s32[4096]{0:T(1024)S(1)}, s32[4096]{0:T(1024)}, u32[]{:S(2)}) %copy-start.1) | copy-done | bytes 16408
  1.4 0.0 copy-start.2
  1.4 0.7 %copy-done.2 = s32[4096]{0:T(1024)S(1)} copy-done((s32[4096]{0:T(1024)S(1)}, s32[4096]{0:T(1024)}, u32[]{:S(2)}) %copy-start.2) | copy-done | bytes 16408
  2.1 0.0 copy-start.3
  2.1 0.7 %copy-done.3 = s32[4096]{0:T(1024)S(1)} copy-done((s32[4096]{0:T(1024)S(1)}, s32[4096]{0:T(1024)}, u32[]{:S(2)}) %copy-start.3) | copy-done | bytes 16408
  2.8 0.0 copy-start.4
  2.8 0.7 %copy-done.4 = f32[1,32,128]{2,1,0:T(8,128)S(1)} copy-done((f32[1,32,128]{2,1,0:T(8,128)S(1)}, f32[1,32,128]{2,1,0:T(8,128)}, u32[]{:S(2)}) %copy-start.4) | copy-done | bytes 16408
  3.5 0.0 copy-start.5
  3.5 0.7 %copy-done.5 = f32[1,32,128]{2,1,0:T(8,128)S(1)} copy-done((f32[1,32,128]{2,1,0:T(8,128)S(1)}, f32[1,32,128]{2,1,0:T(8,128)}, u32[]{:S(2)}) %copy-start.5) | copy-done | bytes 16408
  4.2 0.0 copy-start.6
  4.2 0.7 %copy-done.6 = f32[1,32,128]{2,1,0:T(8,128)S(1)} copy-done((f32[1,32,128]{2,1,0:T(8,128)S(1)}, f32[1,32,128]{2,1,0:T(8,128)}, u32[]{:S(2)}) %copy-start.6) | copy-done | bytes 16408
  4.9 0.0 copy-start.7
  4.9 0.7 %copy-done.7 = s32[4,128]{1,0:T(4,128)S(1)} copy-done((s32[4,128]{1,0:T(4,128)S(1)}, s32[4,128]{1,0:T(4,128)}, u32[]{:S(2)}) %copy-start.7) | copy-done | bytes 2072
  5.6 1.0 %shard_map.103 = (s32[32,128]{1,0:T(8,128)S(1)}, f32[512,128]{1,0:T(8,128)S(1)}, f32[96,256]{1,0:T(8,128)S(1)}, f32[96,128]{1,0:T(8,128)S(1)}, f32[24,128]{1,0:T(8,128)S(1)}) custom-call(s32[32,128]{1,0:T(8,128)S(1)} %bitcast.10, s32[32,128]{1,0:T(8,128)S(1)} %bitcast.11, s32[32,128]{1,0:T(8,128)S(1)} %bitcast.12, f32[32,128]{1,0:T(8,128)S(1)} %bitcast.13, ...), custom_call_target="tpu_custom_call" | custom-call | tf_op jit(solution)/shard_map/pallas_call | solution.py:367
  6.7 0.0 copy-start
  6.7 1.6 %copy-done = f32[1,1,4096,128]{3,2,1,0:T(8,128)S(1)} copy-done((f32[1,1,4096,128]{3,2,1,0:T(8,128)S(1)}, f32[1,1,4096,128]{3,2,1,0:T(8,128)}, u32[]{:S(2)}) %copy-start) | copy-done | bytes 2097176
  8.2 41.5 %shard_map.104 = (f32[32,128]{1,0:T(8,128)S(1)}, f32[32,128]{1,0:T(8,128)S(1)}, f32[32,128]{1,0:T(8,128)S(1)}) custom-call(s32[4096]{0:T(1024)S(1)} %bitcast.9, f32[4096,128]{1,0:T(8,128)S(1)} %bitcast.8, f32[512,128]{1,0:T(8,128)S(1)} %get-tuple-element.9.out_ref, f32[96,256]{1,0:T(8,128)S(1)} %get-tuple-element.10.wsel_ref, ...), custom_call_target="tpu_custom_call" | custom-call | flops 524288 | bytes 2097152 | tf_op jit(solution)/shard_map/pallas_call | solution.py:393
  49.8 0.6 %copy.14 = f32[32,128]{1,0:T(8,128)} copy(f32[32,128]{1,0:T(8,128)S(1)} %get-tuple-element.16) | data formatting | bytes 32768
  50.4 0.6 %copy.15 = f32[32,128]{1,0:T(8,128)} copy(f32[32,128]{1,0:T(8,128)S(1)} %get-tuple-element.17) | data formatting | bytes 32768
  51.0 0.6 %copy.16 = f32[32,128]{1,0:T(8,128)} copy(f32[32,128]{1,0:T(8,128)S(1)} %get-tuple-element.18) | data formatting | bytes 32768
Async XLA Ops:
  0.6 0.7 %copy-start.1 = (s32[4096]{0:T(1024)S(1)}, s32[4096]{0:T(1024)}, u32[]{:S(2)}) copy-start(s32[4096]{0:T(1024)} %param.14) | copy-start | bytes 49156
  1.4 0.7 %copy-start.2 = (s32[4096]{0:T(1024)S(1)}, s32[4096]{0:T(1024)}, u32[]{:S(2)}) copy-start(s32[4096]{0:T(1024)} %param.15) | copy-start | bytes 49156
  2.1 0.7 %copy-start.3 = (s32[4096]{0:T(1024)S(1)}, s32[4096]{0:T(1024)}, u32[]{:S(2)}) copy-start(s32[4096]{0:T(1024)} %param.13) | copy-start | bytes 49156
  2.8 0.7 %copy-start.4 = (f32[1,32,128]{2,1,0:T(8,128)S(1)}, f32[1,32,128]{2,1,0:T(8,128)}, u32[]{:S(2)}) copy-start(f32[1,32,128]{2,1,0:T(8,128)} %param.9) | copy-start | bytes 49156
  3.5 0.7 %copy-start.5 = (f32[1,32,128]{2,1,0:T(8,128)S(1)}, f32[1,32,128]{2,1,0:T(8,128)}, u32[]{:S(2)}) copy-start(f32[1,32,128]{2,1,0:T(8,128)} %param.10) | copy-start | bytes 49156
  4.2 0.7 %copy-start.6 = (f32[1,32,128]{2,1,0:T(8,128)S(1)}, f32[1,32,128]{2,1,0:T(8,128)}, u32[]{:S(2)}) copy-start(f32[1,32,128]{2,1,0:T(8,128)} %param.11) | copy-start | bytes 49156
  4.9 0.7 %copy-start.7 = (s32[4,128]{1,0:T(4,128)S(1)}, s32[4,128]{1,0:T(4,128)}, u32[]{:S(2)}) copy-start(s32[4,128]{1,0:T(4,128)} %lost_ref.1) | copy-start | bytes 6148
  6.7 1.6 %copy-start = (f32[1,1,4096,128]{3,2,1,0:T(8,128)S(1)}, f32[1,1,4096,128]{3,2,1,0:T(8,128)}, u32[]{:S(2)}) copy-start(f32[1,1,4096,128]{3,2,1,0:T(8,128)} %param.8) | copy-start | bytes 6291460

commit v2 on v1

--- a/solution.py
+++ b/solution.py
@@ -22,6 +22,7 @@
 JR = 8
 LANES = 128
 UNROLL = 32
+VMEM_BYTES = 63 * 2**20
 
 MESH = pl.DeviceIdType.MESH
 F32 = jnp.float32
@@ -51,27 +52,9 @@
     return total + jnp.dot(onehot, parts[0], preferred_element_type=F32)
 
 
-def prepare(owner_ref, slot_ref, source_ref, m_ref, v_ref, w_ref, lost_ref,
-            order_ref, out_ref, wsel_ref, stay_ref, aux_ref, held):
-    blk = NX * JR
-    segs = LANES // blk
+def prepare_order(owner_ref, slot_ref, order_ref):
     rows = owner_ref.shape[0]
     zh = NZ // 2
-    x = lax.axis_index("replica")
-    dp = lax.axis_index("dp")
-    y = dp // (2 * NZ)
-    c = dp % 2
-    partner = dp + 1 - 2 * c
-
-    living = (1 - lost_ref[...]).astype(F32)
-    at_row = iota(living.shape, 0)
-    at_col = iota(living.shape, 1)
-    mine = jnp.sum(jnp.where((at_row == x) & (at_col == dp), living, 0.0))
-    other = jnp.sum(jnp.where((at_row == x) & (at_col == partner), living, 0.0))
-    aux_ref[0:8, :] = jnp.full((8, LANES), mine, F32)
-    aux_ref[8:16, :] = jnp.full((8, LANES), other, F32)
-    aux_ref[16:24, :] = jnp.full((8, LANES), jnp.sum(living), F32)
-
     owner = owner_ref[...]
     slot = slot_ref[...]
     oy = owner >> log2(2 * NZ)
@@ -104,6 +87,27 @@
     order = both[:row_pad] * 64.0 + both[row_pad:]
     order_ref[...] = order[:rows].astype(I32)
 
+
+def prepare_state(owner_ref, slot_ref, source_ref, m_ref, v_ref, w_ref, lost_ref,
+                  out_ref, wsel_ref, stay_ref, aux_ref, held):
+    blk = NX * JR
+    segs = LANES // blk
+    x = lax.axis_index("replica")
+    dp = lax.axis_index("dp")
+    y = dp // (2 * NZ)
+    c = dp % 2
+    partner = dp + 1 - 2 * c
+    lane = iota((1, LANES), 1)
+
+    living = (1 - lost_ref[...]).astype(F32)
+    at_row = iota(living.shape, 0)
+    at_col = iota(living.shape, 1)
+    mine = jnp.sum(jnp.where((at_row == x) & (at_col == dp), living, 0.0))
+    other = jnp.sum(jnp.where((at_row == x) & (at_col == partner), living, 0.0))
+    aux_ref[0:8, :] = jnp.full((8, LANES), mine, F32)
+    aux_ref[8:16, :] = jnp.full((8, LANES), other, F32)
+    aux_ref[16:24, :] = jnp.full((8, LANES), jnp.sum(living), F32)
+
     seg = dp % segs
     held[...] = jnp.zeros_like(held)
     at = pl.ds(pl.multiple_of(seg * blk, 8), blk)
@@ -162,11 +166,18 @@
     wsel_ref[...] = jnp.where((slots == wanted) & (sub == 3 * c + kind), 1.0, 0.0)
 
 
-def exchange(order, grad_hbm, out_ref, wsel_ref, stay_ref, aux_ref,
-             first_ref, second_ref, weight_ref,
-             grad, csend, crecv, own, rx0, rx1, t0, t1, ry0, ry1, u, rz, gfull,
+def prepare(owner_ref, slot_ref, source_ref, m_ref, v_ref, w_ref, lost_ref,
+            order_ref, out_ref, wsel_ref, stay_ref, aux_ref, held):
+    prepare_order(owner_ref, slot_ref, order_ref)
+    prepare_state(owner_ref, slot_ref, source_ref, m_ref, v_ref, w_ref, lost_ref,
+                  out_ref, wsel_ref, stay_ref, aux_ref, held)
+
+
+def exchange(order_hbm, out_hbm, wsel_hbm, stay_hbm, aux_hbm, grad_hbm, result_ref,
+             order, out_ref, wsel_ref, stay_ref, aux_ref,
+             grad, csend, crecv, own, rl0, rl1, rx0, rx1, t0, t1, ry0, ry1, u, rz, gfull,
              srecv, ssum, r1, r2, r3, pbuf, precv,
-             grad_sem, csend_sem, crecv_sem, send_sem, recv_sem):
+             grad_sem, in_sem, csend_sem, crecv_sem, send_sem, recv_sem):
     blk = NX * JR
     zh = NZ // 2
     chunk = NY * zh * JR
@@ -183,6 +194,11 @@
         to_c = (c + dc) % 2
         return ((to_y * NZ + to_z) * 2 + to_c, (x + dx) % NX)
 
+    pairs = ((order_hbm, order), (out_hbm, out_ref), (wsel_hbm, wsel_ref),
+             (stay_hbm, stay_ref), (aux_hbm, aux_ref))
+    small = [pltpu.make_async_copy(src, dst, in_sem.at[i]) for i, (src, dst) in enumerate(pairs)]
+    for copy in small:
+        copy.start()
     load = pltpu.make_async_copy(grad_hbm, grad, grad_sem)
     load.start()
 
@@ -209,7 +225,8 @@
     def gather(dst, dst_base, base):
         def step(i, carry):
             at = base + i * UNROLL
-            values = [grad[pl.ds(order[at + k], 1), :] for k in range(UNROLL)]
+            row, col = at // LANES, at % LANES
+            values = [grad[pl.ds(order[row, col + k], 1), :] for k in range(UNROLL)]
             tile = dst.at[pl.ds(pl.multiple_of(dst_base + i * UNROLL, UNROLL), UNROLL)]
             for k in range(UNROLL):
                 tile[k:k + 1, :] = values[k]
@@ -217,10 +234,12 @@
         lax.fori_loop(0, chunk // UNROLL, step, 0)
 
     chunks = []
-    for k in [2, 1, 3, 0] if NX == 4 else [1, 0]:
+    for k in (2, 1, 3, 0):
         chunks.append((0, k, pl.multiple_of(((x + k) % NX) * chunk, chunk)))
         chunks.append((1, k, pl.multiple_of((NX + (y + k) % NY) * chunk, chunk)))
 
+    for copy in small:
+        copy.wait()
     load.wait()
     core_rows = 2 * NX * chunk
     for i, (h, k, base) in enumerate(chunks):
@@ -242,10 +261,24 @@
         rows = pl.ds(base, chunk)
         await_bytes(crecv.at[rows], crecv_sem.at[i])
         own[rows, :] = own[rows, :] * alive_mine + crecv[rows, :] * alive_other
-        if k > 0:
-            to = device(dx=k) if h == 0 else device(dy=k)
-            send(own.at[rows], (rx0 if h == 0 else rx1).at[k - 1], to,
-                 send_sem.at[1 + h], recv_sem.at[1 + h])
+        relay, landing = (rl0, rx0) if h == 0 else (rl1, rx1)
+        up = device(dx=1) if h == 0 else device(dy=1)
+        down = device(dx=-1) if h == 0 else device(dy=-1)
+        part = chunk // 2
+        low, high = pl.ds(base, part), pl.ds(pl.multiple_of(base + part, part), part)
+        if k == 2:
+            send(own.at[low], relay.at[0], up, send_sem.at[11 + 2 * h], recv_sem.at[11 + 2 * h])
+            send(own.at[high], relay.at[1], down, send_sem.at[12 + 2 * h], recv_sem.at[12 + 2 * h])
+        elif k == 1:
+            send(own.at[high], landing.at[0, part:chunk], up, send_sem.at[1 + h], recv_sem.at[1 + h])
+            await_bytes(relay.at[0], recv_sem.at[11 + 2 * h])
+            own[low, :] = own[low, :] + relay[0]
+            send(own.at[low], landing.at[0, 0:part], up, send_sem.at[1 + h], recv_sem.at[1 + h])
+        elif k == 3:
+            send(own.at[low], landing.at[1, 0:part], down, send_sem.at[1 + h], recv_sem.at[1 + h])
+            await_bytes(relay.at[1], recv_sem.at[12 + 2 * h])
+            own[high, :] = own[high, :] + relay[1]
+            send(own.at[high], landing.at[1, part:chunk], down, send_sem.at[1 + h], recv_sem.at[1 + h])
         if i == len(chunks) // 2:
             await_bytes(srecv, recv_sem.at[0])
             total = out_ref[pl.ds(pl.multiple_of(partner_y * NZ * 8, NZ * 8), NZ * 8), :]
@@ -265,18 +298,12 @@
     own0 = pl.multiple_of(x * chunk, chunk)
     own1 = pl.multiple_of((NX + y) * chunk, chunk)
     await_bytes(rx0, recv_sem.at[1])
-    total = own[pl.ds(own0, chunk), :]
-    for k in range(NX - 1):
-        total = total + rx0[k]
-    t0[...] = total
+    t0[...] = own[pl.ds(own0, chunk), :] + rx0[0] + rx0[1]
     for k in range(1, NY):
         at = pl.ds(pl.multiple_of(((y + k) % NY) * piece, piece), piece)
         send(t0.at[at], ry0.at[k - 1], device(dy=k), send_sem.at[4], recv_sem.at[4])
     await_bytes(rx1, recv_sem.at[2])
-    total = own[pl.ds(own1, chunk), :]
-    for k in range(NY - 1):
-        total = total + rx1[k]
-    t1[...] = total
+    t1[...] = own[pl.ds(own1, chunk), :] + rx1[0] + rx1[1]
     for k in range(1, NX):
         at = pl.ds(pl.multiple_of(((x + k) % NX) * piece, piece), piece)
         send(t1.at[at], ry1.at[k - 1], device(dx=k), send_sem.at[5], recv_sem.at[5])
@@ -338,23 +365,25 @@
     for k in range(NX - 1):
         state = state + precv[k]
     await_bytes(gfull.at[0:NX - 1], recv_sem.at[10])
-    gradient = gfull[...].reshape(blk, LANES) / aux_ref[16:17, :]
-    first = BETA_ONE * state[0:blk] + (1.0 - BETA_ONE) * gradient
-    second = BETA_TWO * state[blk:2 * blk] + (1.0 - BETA_TWO) * gradient * gradient
-    weight = state[2 * blk:3 * blk]
-    update = first / BIAS_FIRST / (jnp.sqrt(second / BIAS_SECOND) + EPSILON)
-    first_ref[...] = first
-    second_ref[...] = second
-    weight_ref[...] = weight - LEARN_RATE * (update + DECAY_RATE * weight)
+    result_ref[0:3 * blk, :] = state
+    result_ref[3 * blk:4 * blk, :] = gfull[...].reshape(blk, LANES) / aux_ref[16:17, :]
 
     await_bytes(csend, csend_sem)
-    for ref, n in ((srecv, 0), (rx0, 1), (rx1, 2), (r1.at[0:NZ - 1], 3), (ry0, 4), (ry1, 5),
+    for ref, n in ((srecv, 0), (rx0, 1), (rx1, 2),
+                   (rl0.at[0], 11), (rl0.at[1], 12), (rl1.at[0], 13), (rl1.at[1], 14), (r1.at[0:NZ - 1], 3), (ry0, 4), (ry1, 5),
                    (rz, 7), (r3, 8), (precv, 9), (gfull.at[0:NX - 1], 10)):
         await_bytes(ref, send_sem.at[n])
 
     @pl.when(partner_y != y)
     def _():
         await_bytes(r1, send_sem.at[6])
+
+
+def adamw_update(moment_one, moment_two, weight, gradient_rows):
+    first = BETA_ONE * moment_one + (1.0 - BETA_ONE) * gradient_rows
+    second = BETA_TWO * moment_two + (1.0 - BETA_TWO) * gradient_rows * gradient_rows
+    update = first / BIAS_FIRST / (jnp.sqrt(second / BIAS_SECOND) + EPSILON)
+    return (first, second, weight - LEARN_RATE * (update + DECAY_RATE * weight))
 
 
 def on_device(grad_local, first_moment, second_moment, master_weight, lost_rows, source,
@@ -363,23 +392,6 @@
     nblk = new_owner.shape[0]
     rows = nblk // LANES
     half_z = NZ * 8
-    vmem = pl.BlockSpec(memory_space=pltpu.VMEM)
-    order, out, wsel, stay, aux = pl.pallas_call(
-        prepare,
-        out_shape=(
-            jax.ShapeDtypeStruct((rows, LANES), I32),
-            jax.ShapeDtypeStruct((NY * half_z, LANES), F32),
-            jax.ShapeDtypeStruct((3 * blk, 2 * half_z), F32),
-            jax.ShapeDtypeStruct((3 * blk, LANES), F32),
-            jax.ShapeDtypeStruct((24, LANES), F32),
-        ),
-        in_specs=[vmem] * 7,
-        out_specs=[vmem] * 5,
-        scratch_shapes=[pltpu.VMEM((LANES, 3 * LANES), F32)],
-        compiler_params=pltpu.CompilerParams(vmem_limit_bytes=24 * 2**20),
-    )(new_owner.reshape(rows, LANES), new_slot.reshape(rows, LANES), source.reshape(rows, LANES),
-      first_moment[0], second_moment[0], master_weight[0], lost_rows)
-
     zh = NZ // 2
     chunk = NY * zh * JR
     piece = zh * JR
@@ -388,28 +400,46 @@
     def buf(*shape):
         return pltpu.VMEM(shape + (LANES,), F32)
 
+    def whole(*shape):
+        return pl.BlockSpec(shape, lambda i: (0, 0))
+
+    table = (rows, LANES)
+    shapes = ((NY * half_z, LANES), (3 * blk, 2 * half_z), (3 * blk, LANES), (24, LANES))
+    prepared = pl.pallas_call(
+        prepare,
+        grid=(1,),
+        out_shape=[jax.ShapeDtypeStruct(table, I32)]
+        + [jax.ShapeDtypeStruct(shape, F32) for shape in shapes],
+        in_specs=[whole(*table)] * 3 + [whole(blk, LANES)] * 3 + [whole(*lost_rows.shape)],
+        out_specs=[whole(*table)] + [whole(*shape) for shape in shapes],
+        scratch_shapes=[pltpu.VMEM((LANES, 3 * LANES), F32)],
+        compiler_params=pltpu.CompilerParams(vmem_limit_bytes=VMEM_BYTES),
+    )(new_owner.reshape(table), new_slot.reshape(table), source.reshape(table),
+      first_moment[0], second_moment[0], master_weight[0], lost_rows)
     dma = pltpu.SemaphoreType.DMA
-    result = jax.ShapeDtypeStruct((blk, LANES), F32)
-    return pl.pallas_call(
+    result = pl.pallas_call(
         exchange,
-        out_shape=(result,) * 3,
-        in_specs=[pl.BlockSpec(memory_space=pltpu.SMEM), pl.BlockSpec(memory_space=pl.ANY)]
-        + [vmem] * 4,
-        out_specs=[vmem] * 3,
+        out_shape=jax.ShapeDtypeStruct((4 * blk, LANES), F32),
+        in_specs=[pl.BlockSpec(memory_space=pl.ANY)] * 6,
+        out_specs=pl.BlockSpec(memory_space=pltpu.VMEM),
         scratch_shapes=[
+            pltpu.SMEM(table, I32), *[pltpu.VMEM(shape, F32) for shape in shapes],
             buf(nblk), buf(half_rows), buf(half_rows), buf(half_rows),
-            buf(NX - 1, chunk), buf(NY - 1, chunk), buf(chunk), buf(chunk),
+            buf(2, chunk // 2), buf(2, chunk // 2),
+            buf(2, chunk), buf(2, chunk), buf(chunk), buf(chunk),
             buf(NY - 1, piece), buf(NX - 1, piece), buf(2 * piece),
             buf(NZ - 1, JR), buf(NX, JR),
             buf(NX - 1, half_z), buf(half_z), buf(NZ, 8), buf(NZ, 8), buf(NZ, 8),
             buf(3 * blk), buf(NX - 1, 3 * blk),
-            dma, dma, dma((2 * NX,)), dma((11,)), dma((11,)),
+            dma, dma((5,)), dma, dma((2 * NX,)), dma((15,)), dma((15,)),
         ],
         compiler_params=pltpu.CompilerParams(
-            collective_id=0, has_side_effects=True, vmem_limit_bytes=32 * 2**20),
+            collective_id=0, has_side_effects=True, vmem_limit_bytes=VMEM_BYTES),
         cost_estimate=pl.CostEstimate(
             flops=nblk * LANES, bytes_accessed=nblk * LANES * 4, transcendentals=0),
-    )(order.reshape(nblk), grad_local[0, 0], out, wsel, stay, aux)
+    )(*prepared, grad_local[0, 0])
+    return adamw_update(result[0:blk], result[blk:2 * blk], result[2 * blk:3 * blk],
+                        result[3 * blk:4 * blk])
 
 
 def solution(mesh):

time: 52.6 us -> 51.9 us (0.987)
  local copies, waits for them, and re-layouts: 8.38 us -> 0 us
  Pallas kernels: 42.5 us -> 49.1 us
  other arithmetic: 0 us -> 1.4 us
    unnamed x19 -> x0, local copies, waits for them, and re-layouts: 8.38 us -> none
    pallas_call x2, Pallas kernels: 42.5 us -> 49.1 us  [the longest x1 46.6 us: on_device(): pl.pallas_call(exchange, out_shape=jax.ShapeDtypeStruct((4 * blk, LANES),...]
    sub x0 -> x1, other arithmetic: none -> 1.4 us  [adamw_update(): return (first, second, weight - LEARN_RATE * (update + DECAY_RATE * weight))]
where the time goes in v2:
time: 51.9 us; the launch traced here: 51.2 us
  Pallas kernels  49.1 us (95%)
  other arithmetic  1.4 us (3%)
  between operations  0.64 us (1%)
    pallas_call x1, Pallas kernels, on_device(): pl.pallas_call(exchange, out_shape=jax.ShapeDtypeStruct((4 * blk, LANES),...  46.6 us
    pallas_call x1, Pallas kernels, on_device(): pl.pallas_call(prepare, grid=(1,), out_shape=[jax.ShapeDtypeStruct(table,...  2.56 us
    sub x1, other arithmetic, adamw_update(): return (first, second, weight - LEARN_RATE * (update + DECAY_RATE * weight))  1.4 us

profile of v2, /device:TPU:24, one launch (start us, length us, event | category | flops | bytes accessed | tf_op | source)
XLA Modules:
  0.0 51.2 jit_solution(4253590029060096963)
XLA Ops:
  0.6 2.6 %shard_map.103 = (s32[32,128]{1,0:T(8,128)}, f32[512,128]{1,0:T(8,128)}, f32[96,256]{1,0:T(8,128)}, f32[96,128]{1,0:T(8,128)}, f32[24,128]{1,0:T(8,128)}) custom-call(s32[32,128]{1,0:T(8,128)} %bitcast.8, s32[32,128]{1,0:T(8,128)} %bitcast.9, s32[32,128]{1,0:T(8,128)} %bitcast.10, f32[32,128]{1,0:T(8,128)} %bitcast.11, f32[32,128]{1,0:T(8,128)} %bitcast.12, ...), custom_call_target="tpu_custom_call" | custom-call | tf_op jit(solution)/shard_map/pallas_call | solution.py:408
  3.2 46.6 %shard_map.104 = f32[128,128]{1,0:T(8,128)} custom-call(s32[32,128]{1,0:T(8,128)} %get-tuple-element.8.order_hbm, f32[512,128]{1,0:T(8,128)} %get-tuple-element.9.out_hbm, f32[96,256]{1,0:T(8,128)} %get-tuple-element.10.wsel_hbm, f32[96,128]{1,0:T(8,128)} %get-tuple-element.11.stay_hbm, f32[24,128]{1,0:T(8,128)} %get-tuple-element.12.aux_hbm, ...), custom_call_target="tpu_custom_call" | custom-call | flops 524288 | bytes 2097152 | tf_op jit(solution)/shard_map/pallas_call | solution.py:420
  49.8 1.4 %multiply_subtract_fusion = (f32[32,128]{1,0:T(8,128)}, f32[32,128]{1,0:T(8,128)}, f32[32,128]{1,0:T(8,128)}) fusion(f32[128,128]{1,0:T(8,128)} %shard_map.104), kind=kLoop, calls=%fused_computation.2 | loop fusion | flops 61440 | bytes 114688 | tf_op jit(solution)/shard_map/sub | solution.py:386

commit v3 on v2

--- a/solution.py
+++ b/solution.py
@@ -222,15 +222,18 @@
     def await_bytes(ref, sem):
         pltpu.make_async_copy(ref, ref, sem).wait()
 
+    grad_rows = grad.reshape(grad.shape[0], 1, LANES)
+
     def gather(dst, dst_base, base):
+        dst_rows = dst.reshape(dst.shape[0], 1, LANES)
+
         def step(i, carry):
-            at = base + i * UNROLL
-            row, col = at // LANES, at % LANES
-            values = [grad[pl.ds(order[row, col + k], 1), :] for k in range(UNROLL)]
-            tile = dst.at[pl.ds(pl.multiple_of(dst_base + i * UNROLL, UNROLL), UNROLL)]
+            at = i * UNROLL
+            values = [grad_rows[order[base + at + k]] for k in range(UNROLL)]
             for k in range(UNROLL):
-                tile[k:k + 1, :] = values[k]
+                dst_rows[dst_base + at + k] = values[k]
             return carry
+
         lax.fori_loop(0, chunk // UNROLL, step, 0)
 
     chunks = []
@@ -256,29 +259,39 @@
     alive_mine = aux_ref[0:1, :]
     alive_other = aux_ref[8:9, :]
     partner_y = (x - y + NX) % NX
+    part = chunk // 2
+    relays, landings = (rl0, rl1), (rx0, rx1)
+
+    def pass_on(i):
+        h, k, base = chunks[i]
+        axis = "dx" if h == 0 else "dy"
+        side = 0 if k == 1 else 1
+        rows = pl.ds(pl.multiple_of(base + side * part, part), part)
+        await_bytes(relays[h].at[side], recv_sem.at[11 + 2 * h + side])
+        own[rows, :] = own[rows, :] + relays[h][side]
+        send(own.at[rows], landings[h].at[side, side * part:(side + 1) * part],
+             device(**{axis: 1 - 2 * side}), send_sem.at[1 + h], recv_sem.at[1 + h])
+
     for i, (h, k, base) in enumerate(chunks):
         gather(own, base, c * core_rows + base)
         rows = pl.ds(base, chunk)
         await_bytes(crecv.at[rows], crecv_sem.at[i])
         own[rows, :] = own[rows, :] * alive_mine + crecv[rows, :] * alive_other
-        relay, landing = (rl0, rx0) if h == 0 else (rl1, rx1)
-        up = device(dx=1) if h == 0 else device(dy=1)
-        down = device(dx=-1) if h == 0 else device(dy=-1)
-        part = chunk // 2
-        low, high = pl.ds(base, part), pl.ds(pl.multiple_of(base + part, part), part)
+        axis = "dx" if h == 0 else "dy"
+        low = pl.ds(base, part)
+        high = pl.ds(pl.multiple_of(base + part, part), part)
+        up, down = device(**{axis: 1}), device(**{axis: -1})
+        relay, landing = relays[h], landings[h]
+        straight = (send_sem.at[1 + h], recv_sem.at[1 + h])
         if k == 2:
             send(own.at[low], relay.at[0], up, send_sem.at[11 + 2 * h], recv_sem.at[11 + 2 * h])
             send(own.at[high], relay.at[1], down, send_sem.at[12 + 2 * h], recv_sem.at[12 + 2 * h])
         elif k == 1:
-            send(own.at[high], landing.at[0, part:chunk], up, send_sem.at[1 + h], recv_sem.at[1 + h])
-            await_bytes(relay.at[0], recv_sem.at[11 + 2 * h])
-            own[low, :] = own[low, :] + relay[0]
-            send(own.at[low], landing.at[0, 0:part], up, send_sem.at[1 + h], recv_sem.at[1 + h])
+            send(own.at[high], landing.at[0, part:chunk], up, *straight)
         elif k == 3:
-            send(own.at[low], landing.at[1, 0:part], down, send_sem.at[1 + h], recv_sem.at[1 + h])
-            await_bytes(relay.at[1], recv_sem.at[12 + 2 * h])
-            own[high, :] = own[high, :] + relay[1]
-            send(own.at[high], landing.at[1, part:chunk], down, send_sem.at[1 + h], recv_sem.at[1 + h])
+            send(own.at[low], landing.at[1, 0:part], down, *straight)
+        if i >= 4:
+            pass_on(i - 2)
         if i == len(chunks) // 2:
             await_bytes(srecv, recv_sem.at[0])
             total = out_ref[pl.ds(pl.multiple_of(partner_y * NZ * 8, NZ * 8), NZ * 8), :]
@@ -423,7 +436,7 @@
         in_specs=[pl.BlockSpec(memory_space=pl.ANY)] * 6,
         out_specs=pl.BlockSpec(memory_space=pltpu.VMEM),
         scratch_shapes=[
-            pltpu.SMEM(table, I32), *[pltpu.VMEM(shape, F32) for shape in shapes],
+            pltpu.SMEM((nblk,), I32), *[pltpu.VMEM(shape, F32) for shape in shapes],
             buf(nblk), buf(half_rows), buf(half_rows), buf(half_rows),
             buf(2, chunk // 2), buf(2, chunk // 2),
             buf(2, chunk), buf(2, chunk), buf(chunk), buf(chunk),
@@ -437,7 +450,7 @@
             collective_id=0, has_side_effects=True, vmem_limit_bytes=VMEM_BYTES),
         cost_estimate=pl.CostEstimate(
             flops=nblk * LANES, bytes_accessed=nblk * LANES * 4, transcendentals=0),
-    )(*prepared, grad_local[0, 0])
+    )(prepared[0].reshape(nblk), *prepared[1:], grad_local[0, 0])
     return adamw_update(result[0:blk], result[blk:2 * blk], result[2 * blk:3 * blk],
                         result[3 * blk:4 * blk])
 

time: 51.9 us -> 47.9 us (0.923)
  the two profiles are of different devices: /device:TPU:24 before, /device:TPU:8 now
where the time goes in v3:
time: 47.9 us; the launch traced here: 47.6 us
  Pallas kernels  45.6 us (95%)
  other arithmetic  1.4 us (3%)
  between operations  0.64 us (1%)
    pallas_call x1, Pallas kernels, on_device(): pl.pallas_call(exchange, out_shape=jax.ShapeDtypeStruct((4 * blk, LANES),...  43 us
    pallas_call x1, Pallas kernels, on_device(): pl.pallas_call(prepare, grid=(1,), out_shape=[jax.ShapeDtypeStruct(table,...  2.56 us
    sub x1, other arithmetic, adamw_update(): return (first, second, weight - LEARN_RATE * (update + DECAY_RATE * weight))  1.4 us

profile of v3, /device:TPU:8, one launch (start us, length us, event | category | flops | bytes accessed | tf_op | source)
XLA Modules:
  0.0 47.6 jit_solution(886689582644070396)
XLA Ops:
  0.6 2.6 %shard_map.103 = (s32[32,128]{1,0:T(8,128)}, f32[512,128]{1,0:T(8,128)}, f32[96,256]{1,0:T(8,128)}, f32[96,128]{1,0:T(8,128)}, f32[24,128]{1,0:T(8,128)}) custom-call(s32[32,128]{1,0:T(8,128)} %bitcast.10, s32[32,128]{1,0:T(8,128)} %bitcast.11, s32[32,128]{1,0:T(8,128)} %bitcast.12, f32[32,128]{1,0:T(8,128)} %bitcast.13, f32[32,128]{1,0:T(8,128)} %bitcast.14, ...), custom_call_target="tpu_custom_call" | custom-call | tf_op jit(solution)/shard_map/pallas_call | solution.py:421
  3.2 43.0 %shard_map.104 = f32[128,128]{1,0:T(8,128)} custom-call(s32[4096]{0:T(1024)} %bitcast.9, f32[512,128]{1,0:T(8,128)} %get-tuple-element.9.out_hbm, f32[96,256]{1,0:T(8,128)} %get-tuple-element.10.wsel_hbm, f32[96,128]{1,0:T(8,128)} %get-tuple-element.11.stay_hbm, f32[24,128]{1,0:T(8,128)} %get-tuple-element.12.aux_hbm, f32[4096,128]{1,0:T(8,128)} %bitcast.8), custom_call_target="tpu_custom_call" | custom-call | flops 524288 | bytes 2097152 | tf_op jit(solution)/shard_map/pallas_call | solution.py:433
  46.2 1.4 %multiply_subtract_fusion = (f32[32,128]{1,0:T(8,128)}, f32[32,128]{1,0:T(8,128)}, f32[32,128]{1,0:T(8,128)}) fusion(f32[128,128]{1,0:T(8,128)} %shard_map.104), kind=kLoop, calls=%fused_computation.2 | loop fusion | flops 61440 | bytes 114688 | tf_op jit(solution)/shard_map/sub | solution.py:399

commit v4 on v3

--- a/solution.py
+++ b/solution.py
@@ -245,7 +245,9 @@
         copy.wait()
     load.wait()
     core_rows = 2 * NX * chunk
-    for i, (h, k, base) in enumerate(chunks):
+
+    def for_partner(i):
+        base = chunks[i][2]
         gather(csend, base, (1 - c) * core_rows + base)
         if i == 0:
             pl.semaphore_wait(barrier, len(peers) + NZ - 1)
@@ -272,7 +274,8 @@
         send(own.at[rows], landings[h].at[side, side * part:(side + 1) * part],
              device(**{axis: 1 - 2 * side}), send_sem.at[1 + h], recv_sem.at[1 + h])
 
-    for i, (h, k, base) in enumerate(chunks):
+    def for_me(i):
+        h, k, base = chunks[i]
         gather(own, base, c * core_rows + base)
         rows = pl.ds(base, chunk)
         await_bytes(crecv.at[rows], crecv_sem.at[i])
@@ -290,9 +293,9 @@
             send(own.at[high], landing.at[0, part:chunk], up, *straight)
         elif k == 3:
             send(own.at[low], landing.at[1, 0:part], down, *straight)
-        if i >= 4:
-            pass_on(i - 2)
-        if i == len(chunks) // 2:
+        for earlier in {3: [2], 4: [3], 5: [4, 5]}.get(i, []):
+            pass_on(earlier)
+        if i == 3:
             await_bytes(srecv, recv_sem.at[0])
             total = out_ref[pl.ds(pl.multiple_of(partner_y * NZ * 8, NZ * 8), NZ * 8), :]
             for dx in range(NX - 1):
@@ -307,6 +310,13 @@
                 return carry
 
             lax.fori_loop(1, NZ, spread, 0)
+
+    lag = 3
+    for i in range(len(chunks) + lag):
+        if i < len(chunks):
+            for_partner(i)
+        if i >= lag:
+            for_me(i - lag)
 
     own0 = pl.multiple_of(x * chunk, chunk)
     own1 = pl.multiple_of((NX + y) * chunk, chunk)

time: 47.9 us -> 48.8 us (1.019)
  the two profiles are of different devices: /device:TPU:8 before, /device:TPU:2 now
where the time goes in v4:
time: 48.8 us; the launch traced here: 48.5 us
  Pallas kernels  46.4 us (95%)
  other arithmetic  1.4 us (3%)
  between operations  0.64 us (1%)
    pallas_call x1, Pallas kernels, on_device(): pl.pallas_call(exchange, out_shape=jax.ShapeDtypeStruct((4 * blk, LANES),...  43.9 us
    pallas_call x1, Pallas kernels, on_device(): pl.pallas_call(prepare, grid=(1,), out_shape=[jax.ShapeDtypeStruct(table,...  2.55 us
    sub x1, other arithmetic, adamw_update(): return (first, second, weight - LEARN_RATE * (update + DECAY_RATE * weight))  1.4 us

profile of v4, /device:TPU:2, one launch (start us, length us, event | category | flops | bytes accessed | tf_op | source)
XLA Modules:
  0.0 48.5 jit_solution(10851179079204235796)
XLA Ops:
  0.6 2.6 %shard_map.103 = (s32[32,128]{1,0:T(8,128)}, f32[512,128]{1,0:T(8,128)}, f32[96,256]{1,0:T(8,128)}, f32[96,128]{1,0:T(8,128)}, f32[24,128]{1,0:T(8,128)}) custom-call(s32[32,128]{1,0:T(8,128)} %bitcast.10, s32[32,128]{1,0:T(8,128)} %bitcast.11, s32[32,128]{1,0:T(8,128)} %bitcast.12, f32[32,128]{1,0:T(8,128)} %bitcast.13, f32[32,128]{1,0:T(8,128)} %bitcast.14, ...), custom_call_target="tpu_custom_call" | custom-call | tf_op jit(solution)/shard_map/pallas_call | solution.py:431
  3.2 43.9 %shard_map.104 = f32[128,128]{1,0:T(8,128)} custom-call(s32[4096]{0:T(1024)} %bitcast.9, f32[512,128]{1,0:T(8,128)} %get-tuple-element.9.out_hbm, f32[96,256]{1,0:T(8,128)} %get-tuple-element.10.wsel_hbm, f32[96,128]{1,0:T(8,128)} %get-tuple-element.11.stay_hbm, f32[24,128]{1,0:T(8,128)} %get-tuple-element.12.aux_hbm, f32[4096,128]{1,0:T(8,128)} %bitcast.8), custom_call_target="tpu_custom_call" | custom-call | flops 524288 | bytes 2097152 | tf_op jit(solution)/shard_map/pallas_call | solution.py:443
  47.1 1.4 %multiply_subtract_fusion = (f32[32,128]{1,0:T(8,128)}, f32[32,128]{1,0:T(8,128)}, f32[32,128]{1,0:T(8,128)}) fusion(f32[128,128]{1,0:T(8,128)} %shard_map.104), kind=kLoop, calls=%fused_computation.2 | loop fusion | flops 61440 | bytes 114688 | tf_op jit(solution)/shard_map/sub | solution.py:409

commit v5 on v4

--- a/solution.py
+++ b/solution.py
@@ -89,7 +89,7 @@
 
 
 def prepare_state(owner_ref, slot_ref, source_ref, m_ref, v_ref, w_ref, lost_ref,
-                  out_ref, wsel_ref, stay_ref, aux_ref, held):
+                  masked_ref, wout_ref, wsel_ref, wstay_ref, aux_ref):
     blk = NX * JR
     segs = LANES // blk
     x = lax.axis_index("replica")
@@ -98,6 +98,7 @@
     c = dp % 2
     partner = dp + 1 - 2 * c
     lane = iota((1, LANES), 1)
+    from_y = (x - y + NX) % NX
 
     living = (1 - lost_ref[...]).astype(F32)
     at_row = iota(living.shape, 0)
@@ -109,74 +110,79 @@
     aux_ref[16:24, :] = jnp.full((8, LANES), jnp.sum(living), F32)
 
     seg = dp % segs
-    held[...] = jnp.zeros_like(held)
-    at = pl.ds(pl.multiple_of(seg * blk, 8), blk)
-    keep = jnp.full((blk, LANES), mine, F32) > 0.5
-    held[at, 0:128] = jnp.where(keep, m_ref[...], 0.0)
-    held[at, 128:256] = jnp.where(keep, v_ref[...], 0.0)
-    held[at, 256:384] = jnp.where(keep, w_ref[...], 0.0)
-    parts = three_parts(held[...])
     own_row = dp // segs
     owner_row = owner_ref[pl.ds(own_row, 1), :]
     slot_row = slot_ref[pl.ds(own_row, 1), :]
     source_row = source_ref[pl.ds(own_row, 1), :]
-    here = ((lane >> log2(blk)) == seg) & (source_row == x)
-
-    leaving = jnp.where(here & (owner_row != dp), owner_row, -2)
-    total_rows = NY * NZ * 8
-    at_dest = iota((total_rows, LANES), 0)
-    pair = at_dest >> 3
-    sub = at_dest & 7
-    result = None
-    for k in range(3):
-        dest = jnp.where(sub == k, 2 * pair, jnp.where(sub == 3 + k, 2 * pair + 1, -1))
-        onehot = jnp.where(dest == leaving, 1.0, 0.0).astype(BF16)
-        got = pick(onehot, [p[:, k * 128:(k + 1) * 128] for p in parts])
-        result = got if result is None else result + got
-    out_ref[...] = result
-
-    staying = jnp.where(here & (owner_row == dp), slot_row, -1)
-    onehot = jnp.where(iota((blk, LANES), 0) == staying, 1.0, 0.0).astype(BF16)
-    got = pick(onehot, parts)
-    for k in range(3):
-        stay_ref[k * blk:(k + 1) * blk, :] = got[:, k * 128:(k + 1) * 128]
+    hit = (iota((blk, LANES), 0) + seg * blk == lane) & (source_row == x)
+    mask = jnp.dot(jnp.where(hit, 1.0, 0.0).astype(BF16), jnp.ones((LANES, LANES), BF16),
+                   preferred_element_type=F32)
+    for k, ref in enumerate((m_ref, v_ref, w_ref)):
+        chosen = jnp.where(mask > 0.5, ref[...], 0.0)
+        for q in range(NX):
+            masked_ref[q * 3 * JR + k * JR:q * 3 * JR + (k + 1) * JR, :] = (
+                chosen[q * JR:(q + 1) * JR])
+
+    def quarter(index):
+        return (index * 43) >> 10
+
+    col = iota((LANES, LANES), 1)
+    place = seg * blk + quarter(col) * JR + (col & (JR - 1))
+    spread = jnp.where((iota((LANES, LANES), 0) == place) & (col < 3 * blk), 1.0, 0.0)
+    both = jnp.where(iota((8, LANES), 0) == 0, owner_row + 1, slot_row + 1).astype(F32)
+    both = jnp.dot(both.astype(BF16), spread.astype(BF16), preferred_element_type=F32)
+    owner_at = both[0:1, :].astype(I32)
+    slot_at = both[1:2, :].astype(I32)
+    kind_at = (lane - 24 * quarter(lane)) >> log2(JR)
+
+    leaving = jnp.where(owner_at == dp + 1, -5, owner_at)
+    row = iota((NZ * 8, LANES), 0)
+    sub = row & 7
+    core = jnp.where(sub >= 3, 1, 0)
+    dest = (from_y * NZ + (row >> 3)) * 2 + core + 1
+    wanted = jnp.where(sub < 6, dest, -9)
+    wout_ref[...] = jnp.where((wanted == leaving) & (sub - 3 * core == kind_at), 1.0, 0.0)
+
+    row = iota((3 * JR, LANES), 0)
+    wanted = x * JR + (row & (JR - 1)) + 1
+    wstay_ref[...] = jnp.where(
+        (owner_at == dp + 1) & (slot_at == wanted) & ((row >> log2(JR)) == kind_at), 1.0, 0.0)
 
     group_rows = 2 * NZ * blk // LANES
-    from_y = (x - y + NX) % NX
     at = pl.ds(pl.multiple_of(from_y * group_rows, group_rows), group_rows)
     block = (from_y * group_rows + iota((group_rows, LANES), 0)) * LANES + iota((group_rows, LANES), 1)
     coming = (owner_ref[at, :] == dp) & ((block >> log2(blk)) != dp)
     named = jnp.where(coming, slot_ref[at, :] + 1, 0).astype(F32)
     cols = 2 * NZ * 8
+
     def source_of(shape):
         col = iota(shape, 1)
         core = jnp.where(col >= NZ * 8, 1 - c, c)
         return ((col & (NZ * 8 - 1)) >> 3) * 2 + core
+
     spread = jnp.where(
         (iota((LANES, cols), 0) >> log2(blk)) == (source_of((LANES, cols)) & (segs - 1)), 1.0, 0.0)
-    if group_rows < 8:
-        named = jnp.concatenate([named, jnp.zeros((8 - group_rows, LANES), F32)], axis=0)
     table = jnp.dot(named.astype(BF16), spread.astype(BF16), preferred_element_type=F32)
     row_of = source_of((8, cols)) >> log2(segs)
     slots = jnp.sum(jnp.where(iota((8, cols), 0) == row_of, table, 0.0), axis=0, keepdims=True)
-    at_row = iota((3 * blk, cols), 0)
-    kind = at_row >> log2(blk)
+    row = iota((3 * blk, cols), 0)
+    kind = (row - 24 * quarter(row)) >> log2(JR)
     sub = iota((3 * blk, cols), 1) & 7
-    wanted = ((at_row & (blk - 1)) + 1).astype(F32)
+    wanted = (quarter(row) * JR + (row & (JR - 1)) + 1).astype(F32)
     wsel_ref[...] = jnp.where((slots == wanted) & (sub == 3 * c + kind), 1.0, 0.0)
 
 
 def prepare(owner_ref, slot_ref, source_ref, m_ref, v_ref, w_ref, lost_ref,
-            order_ref, out_ref, wsel_ref, stay_ref, aux_ref, held):
+            order_ref, masked_ref, wout_ref, wsel_ref, wstay_ref, aux_ref):
     prepare_order(owner_ref, slot_ref, order_ref)
     prepare_state(owner_ref, slot_ref, source_ref, m_ref, v_ref, w_ref, lost_ref,
-                  out_ref, wsel_ref, stay_ref, aux_ref, held)
-
-
-def exchange(order_hbm, out_hbm, wsel_hbm, stay_hbm, aux_hbm, grad_hbm, result_ref,
-             order, out_ref, wsel_ref, stay_ref, aux_ref,
+                  masked_ref, wout_ref, wsel_ref, wstay_ref, aux_ref)
+
+
+def exchange(order_hbm, masked_hbm, wout_hbm, wsel_hbm, wstay_hbm, aux_hbm, grad_hbm, result_ref,
+             order, masked_ref, wout_ref, wsel_ref, wstay_ref, aux_ref,
              grad, csend, crecv, own, rl0, rl1, rx0, rx1, t0, t1, ry0, ry1, u, rz, gfull,
-             srecv, ssum, r1, r2, r3, pbuf, precv,
+             srecv, state, ssum, r1, r2, r3, pbuf, precv, sfull,
              grad_sem, in_sem, csend_sem, crecv_sem, send_sem, recv_sem):
     blk = NX * JR
     zh = NZ // 2
@@ -194,8 +200,8 @@
         to_c = (c + dc) % 2
         return ((to_y * NZ + to_z) * 2 + to_c, (x + dx) % NX)
 
-    pairs = ((order_hbm, order), (out_hbm, out_ref), (wsel_hbm, wsel_ref),
-             (stay_hbm, stay_ref), (aux_hbm, aux_ref))
+    pairs = ((order_hbm, order), (masked_hbm, masked_ref), (wout_hbm, wout_ref),
+             (wsel_hbm, wsel_ref), (wstay_hbm, wstay_ref), (aux_hbm, aux_ref))
     small = [pltpu.make_async_copy(src, dst, in_sem.at[i]) for i, (src, dst) in enumerate(pairs)]
     for copy in small:
         copy.start()
@@ -245,6 +251,8 @@
         copy.wait()
     load.wait()
     core_rows = 2 * NX * chunk
+    share = 3 * JR
+    my_share = pl.ds(pl.multiple_of(x * share, share), share)
 
     def for_partner(i):
         base = chunks[i][2]
@@ -252,9 +260,8 @@
         if i == 0:
             pl.semaphore_wait(barrier, len(peers) + NZ - 1)
             for dx in range(1, NX):
-                to_y = (x + dx - y + NX) % NX
-                send(out_ref.at[pl.ds(pl.multiple_of(to_y * NZ * 8, NZ * 8), NZ * 8)],
-                     srecv.at[dx - 1], device(dx=dx), send_sem.at[0], recv_sem.at[0])
+                at = pl.ds(pl.multiple_of(((x + dx) % NX) * share, share), share)
+                send(masked_ref.at[at], srecv.at[dx - 1], device(dx=dx), send_sem.at[0], recv_sem.at[0])
         rows = pl.ds(base, chunk)
         send(csend.at[rows], crecv.at[rows], device(dc=1), csend_sem, crecv_sem.at[i])
 
@@ -295,12 +302,16 @@
             send(own.at[low], landing.at[1, 0:part], down, *straight)
         for earlier in {3: [2], 4: [3], 5: [4, 5]}.get(i, []):
             pass_on(earlier)
-        if i == 3:
+        if i == 0:
             await_bytes(srecv, recv_sem.at[0])
-            total = out_ref[pl.ds(pl.multiple_of(partner_y * NZ * 8, NZ * 8), NZ * 8), :]
-            for dx in range(NX - 1):
-                total = total + srecv[dx]
-            ssum[...] = total
+            state[x] = masked_ref[my_share, :] + srecv[0] + srecv[1] + srecv[2]
+            for dx in range(1, NX):
+                send(state.at[x], state.at[x], device(dx=dx), send_sem.at[15], recv_sem.at[15])
+        if i == 2:
+            await_bytes(state.at[0:NX - 1], recv_sem.at[15])
+            parts = three_parts(state[...].reshape(3 * blk, LANES))
+            ssum[...] = pick(wout_ref[:, 0:3 * blk].astype(BF16), parts)
+            sfull[x] = pick(wstay_ref[:, 0:3 * blk].astype(BF16), parts)
             r1[z] = ssum[pl.ds(pl.multiple_of(z * 8, 8), 8), :]
 
             def spread(kz, carry):
@@ -368,12 +379,17 @@
     send(r2, r3, device(dc=1), send_sem.at[8], recv_sem.at[8])
     half = NZ * 8
     near = three_parts(r2[...].reshape(half, LANES))
-    total = stay_ref[...] + pick(wsel_ref[:, 0:half].astype(BF16), near)
+    total = pick(wsel_ref[:, 0:half].astype(BF16), near)
     await_bytes(r3, recv_sem.at[8])
     far = three_parts(r3[...].reshape(half, LANES))
     pbuf[...] = total + pick(wsel_ref[:, half:2 * half].astype(BF16), far)
     for k in range(1, NX):
-        send(pbuf, precv.at[k - 1], device(dx=k), send_sem.at[9], recv_sem.at[9])
+        at = pl.ds(pl.multiple_of(((x + k) % NX) * share, share), share)
+        send(pbuf.at[at], precv.at[k - 1], device(dx=k), send_sem.at[9], recv_sem.at[9])
+    await_bytes(precv, recv_sem.at[9])
+    sfull[x] = sfull[x] + pbuf[my_share, :] + precv[0] + precv[1] + precv[2]
+    for k in range(1, NX):
+        send(sfull.at[x], sfull.at[x], device(dx=k), send_sem.at[16], recv_sem.at[16])
 
     await_bytes(rz, recv_sem.at[7])
     total = u[pl.ds(pl.multiple_of(z * JR, JR), JR), :]
@@ -383,18 +399,18 @@
     for k in range(1, NX):
         send(gfull.at[x], gfull.at[x], device(dx=k), send_sem.at[10], recv_sem.at[10])
 
-    await_bytes(precv, recv_sem.at[9])
-    state = pbuf[...]
-    for k in range(NX - 1):
-        state = state + precv[k]
+    await_bytes(sfull.at[0:NX - 1], recv_sem.at[16])
+    for q in range(NX):
+        for k in range(3):
+            result_ref[k * blk + q * JR:k * blk + (q + 1) * JR, :] = sfull[q, k * JR:(k + 1) * JR, :]
     await_bytes(gfull.at[0:NX - 1], recv_sem.at[10])
-    result_ref[0:3 * blk, :] = state
     result_ref[3 * blk:4 * blk, :] = gfull[...].reshape(blk, LANES) / aux_ref[16:17, :]
 
     await_bytes(csend, csend_sem)
     for ref, n in ((srecv, 0), (rx0, 1), (rx1, 2),
                    (rl0.at[0], 11), (rl0.at[1], 12), (rl1.at[0], 13), (rl1.at[1], 14), (r1.at[0:NZ - 1], 3), (ry0, 4), (ry1, 5),
-                   (rz, 7), (r3, 8), (precv, 9), (gfull.at[0:NX - 1], 10)):
+                   (rz, 7), (r3, 8), (precv, 9), (gfull.at[0:NX - 1], 10),
+                   (state.at[0:NX - 1], 15), (sfull.at[0:NX - 1], 16)):
         await_bytes(ref, send_sem.at[n])
 
     @pl.when(partner_y != y)
@@ -427,7 +443,7 @@
         return pl.BlockSpec(shape, lambda i: (0, 0))
 
     table = (rows, LANES)
-    shapes = ((NY * half_z, LANES), (3 * blk, 2 * half_z), (3 * blk, LANES), (24, LANES))
+    shapes = ((3 * blk, LANES), (half_z, LANES), (3 * blk, 2 * half_z), (3 * JR, LANES), (24, LANES))
     prepared = pl.pallas_call(
         prepare,
         grid=(1,),
@@ -435,7 +451,6 @@
         + [jax.ShapeDtypeStruct(shape, F32) for shape in shapes],
         in_specs=[whole(*table)] * 3 + [whole(blk, LANES)] * 3 + [whole(*lost_rows.shape)],
         out_specs=[whole(*table)] + [whole(*shape) for shape in shapes],
-        scratch_shapes=[pltpu.VMEM((LANES, 3 * LANES), F32)],
         compiler_params=pltpu.CompilerParams(vmem_limit_bytes=VMEM_BYTES),
     )(new_owner.reshape(table), new_slot.reshape(table), source.reshape(table),
       first_moment[0], second_moment[0], master_weight[0], lost_rows)
@@ -443,7 +458,7 @@
     result = pl.pallas_call(
         exchange,
         out_shape=jax.ShapeDtypeStruct((4 * blk, LANES), F32),
-        in_specs=[pl.BlockSpec(memory_space=pl.ANY)] * 6,
+        in_specs=[pl.BlockSpec(memory_space=pl.ANY)] * 7,
         out_specs=pl.BlockSpec(memory_space=pltpu.VMEM),
         scratch_shapes=[
             pltpu.SMEM((nblk,), I32), *[pltpu.VMEM(shape, F32) for shape in shapes],
@@ -452,9 +467,9 @@
             buf(2, chunk), buf(2, chunk), buf(chunk), buf(chunk),
             buf(NY - 1, piece), buf(NX - 1, piece), buf(2 * piece),
             buf(NZ - 1, JR), buf(NX, JR),
-            buf(NX - 1, half_z), buf(half_z), buf(NZ, 8), buf(NZ, 8), buf(NZ, 8),
-            buf(3 * blk), buf(NX - 1, 3 * blk),
-            dma, dma((5,)), dma, dma((2 * NX,)), dma((15,)), dma((15,)),
+            buf(NX - 1, 3 * JR), buf(NX, 3 * JR), buf(half_z), buf(NZ, 8), buf(NZ, 8), buf(NZ, 8),
+            buf(3 * blk), buf(NX - 1, 3 * JR), buf(NX, 3 * JR),
+            dma, dma((6,)), dma, dma((2 * NX,)), dma((17,)), dma((17,)),
         ],
         compiler_params=pltpu.CompilerParams(
             collective_id=0, has_side_effects=True, vmem_limit_bytes=VMEM_BYTES),

time: 48.8 us -> 49.1 us (level)
  the two profiles are of different devices: /device:TPU:2 before, /device:TPU:1 now
where the time goes in v5:
time: 49.1 us; the launch traced here: 48.7 us
  Pallas kernels  46.7 us (95%)
  other arithmetic  1.4 us (3%)
  between operations  0.64 us (1%)
    pallas_call x1, Pallas kernels, on_device(): pl.pallas_call(exchange, out_shape=jax.ShapeDtypeStruct((4 * blk, LANES),...  44.7 us
    pallas_call x1, Pallas kernels, on_device(): pl.pallas_call(prepare, grid=(1,), out_shape=[jax.ShapeDtypeStruct(table,...  1.98 us
    sub x1, other arithmetic, adamw_update(): return (first, second, weight - LEARN_RATE * (update + DECAY_RATE * weight))  1.4 us

profile of v5, /device:TPU:1, one launch (start us, length us, event | category | flops | bytes accessed | tf_op | source)
XLA Modules:
  0.0 48.7 jit_solution(6726672645212407508)
XLA Ops:
  0.6 2.0 %shard_map.103 = (s32[32,128]{1,0:T(8,128)}, f32[96,128]{1,0:T(8,128)}, f32[128,128]{1,0:T(8,128)}, f32[96,256]{1,0:T(8,128)}, f32[24,128]{1,0:T(8,128)}, /*index=5*/f32[24,128]{1,0:T(8,128)}) custom-call(s32[32,128]{1,0:T(8,128)} %bitcast.10, s32[32,128]{1,0:T(8,128)} %bitcast.11, s32[32,128]{1,0:T(8,128)} %bitcast.12, f32[32,128]{1,0:T(8,128)} %bitcast.13, ...), custom_call_target="tpu_custom_call" | custom-call | tf_op jit(solution)/shard_map/pallas_call | solution.py:447
  2.6 44.7 %shard_map.104 = f32[128,128]{1,0:T(8,128)} custom-call(s32[4096]{0:T(1024)} %bitcast.9, f32[96,128]{1,0:T(8,128)} %get-tuple-element.10.masked_hbm, f32[128,128]{1,0:T(8,128)} %get-tuple-element.11.wout_hbm, f32[96,256]{1,0:T(8,128)} %get-tuple-element.12.wsel_hbm, f32[24,128]{1,0:T(8,128)} %get-tuple-element.13.wstay_hbm, ...), custom_call_target="tpu_custom_call" | custom-call | flops 524288 | bytes 2097152 | tf_op jit(solution)/shard_map/pallas_call | solution.py:458
  47.3 1.4 %multiply_subtract_fusion = (f32[32,128]{1,0:T(8,128)}, f32[32,128]{1,0:T(8,128)}, f32[32,128]{1,0:T(8,128)}) fusion(f32[128,128]{1,0:T(8,128)} %shard_map.104), kind=kLoop, calls=%fused_computation.2 | loop fusion | flops 61440 | bytes 114688 | tf_op jit(solution)/shard_map/sub | solution.py:425

commit v6 on v5

--- a/solution.py
+++ b/solution.py
@@ -182,7 +182,7 @@
 def exchange(order_hbm, masked_hbm, wout_hbm, wsel_hbm, wstay_hbm, aux_hbm, grad_hbm, result_ref,
              order, masked_ref, wout_ref, wsel_ref, wstay_ref, aux_ref,
              grad, csend, crecv, own, rl0, rl1, rx0, rx1, t0, t1, ry0, ry1, u, rz, gfull,
-             srecv, state, ssum, r1, r2, r3, pbuf, precv, sfull,
+             srecv, state, ssum, r2, r3, pbuf, precv, sfull,
              grad_sem, in_sem, csend_sem, crecv_sem, send_sem, recv_sem):
     blk = NX * JR
     zh = NZ // 2
@@ -219,6 +219,16 @@
         return carry
 
     lax.fori_loop(1, NZ, greet, 0)
+    partner_y = (x - y + NX) % NX
+
+    @pl.when(partner_y != y)
+    def _():
+        def greet_far(to_z, carry):
+            pl.semaphore_signal(barrier, inc=1, device_id=((partner_y * NZ + to_z) * 2 + c, x),
+                                device_id_type=MESH)
+            return carry
+
+        lax.fori_loop(0, NZ, greet_far, 0)
 
     def send(src, dst, to, s_sem, r_sem):
         pltpu.make_async_remote_copy(
@@ -258,7 +268,8 @@
         base = chunks[i][2]
         gather(csend, base, (1 - c) * core_rows + base)
         if i == 0:
-            pl.semaphore_wait(barrier, len(peers) + NZ - 1)
+            pl.semaphore_wait(
+                barrier, len(peers) + NZ - 1 + jnp.where(partner_y != y, NZ, 0).astype(I32))
             for dx in range(1, NX):
                 at = pl.ds(pl.multiple_of(((x + dx) % NX) * share, share), share)
                 send(masked_ref.at[at], srecv.at[dx - 1], device(dx=dx), send_sem.at[0], recv_sem.at[0])
@@ -267,7 +278,6 @@
 
     alive_mine = aux_ref[0:1, :]
     alive_other = aux_ref[8:9, :]
-    partner_y = (x - y + NX) % NX
     part = chunk // 2
     relays, landings = (rl0, rl1), (rx0, rx1)
 
@@ -302,25 +312,32 @@
             send(own.at[low], landing.at[1, 0:part], down, *straight)
         for earlier in {3: [2], 4: [3], 5: [4, 5]}.get(i, []):
             pass_on(earlier)
-        if i == 0:
+        if i == 2:
             await_bytes(srecv, recv_sem.at[0])
             state[x] = masked_ref[my_share, :] + srecv[0] + srecv[1] + srecv[2]
             for dx in range(1, NX):
                 send(state.at[x], state.at[x], device(dx=dx), send_sem.at[15], recv_sem.at[15])
-        if i == 2:
+        if i == 5:
             await_bytes(state.at[0:NX - 1], recv_sem.at[15])
             parts = three_parts(state[...].reshape(3 * blk, LANES))
             ssum[...] = pick(wout_ref[:, 0:3 * blk].astype(BF16), parts)
             sfull[x] = pick(wstay_ref[:, 0:3 * blk].astype(BF16), parts)
-            r1[z] = ssum[pl.ds(pl.multiple_of(z * 8, 8), 8), :]
 
             def spread(kz, carry):
                 to_z = (z + kz) % NZ
-                send(ssum.at[pl.ds(pl.multiple_of(to_z * 8, 8), 8)], r1.at[z],
-                     device(dz=kz), send_sem.at[3], recv_sem.at[3])
+                send(ssum.at[pl.ds(pl.multiple_of(to_z * 8, 8), 8)], r2.at[z],
+                     ((partner_y * NZ + to_z) * 2 + c, x), send_sem.at[3], recv_sem.at[3])
                 return carry
 
             lax.fori_loop(1, NZ, spread, 0)
+
+            @pl.when(partner_y != y)
+            def _():
+                spread(0, 0)
+
+            @pl.when(partner_y == y)
+            def _():
+                r2[z] = ssum[pl.ds(pl.multiple_of(z * 8, 8), 8), :]
 
     lag = 3
     for i in range(len(chunks) + lag):
@@ -342,17 +359,6 @@
         at = pl.ds(pl.multiple_of(((x + k) % NX) * piece, piece), piece)
         send(t1.at[at], ry1.at[k - 1], device(dx=k), send_sem.at[5], recv_sem.at[5])
 
-    await_bytes(r1.at[0:NZ - 1], recv_sem.at[3])
-    partner = ((partner_y * NZ + z) * 2 + c, x)
-
-    @pl.when(partner_y != y)
-    def _():
-        send(r1, r2, partner, send_sem.at[6], recv_sem.at[6])
-
-    @pl.when(partner_y == y)
-    def _():
-        r2[...] = r1[...]
-
     await_bytes(ry0, recv_sem.at[4])
     total = t0[pl.ds(pl.multiple_of(y * piece, piece), piece), :]
     for k in range(NY - 1):
@@ -374,7 +380,11 @@
 
     @pl.when(partner_y != y)
     def _():
-        await_bytes(r2, recv_sem.at[6])
+        await_bytes(r2, recv_sem.at[3])
+
+    @pl.when(partner_y == y)
+    def _():
+        await_bytes(r2.at[0:NZ - 1], recv_sem.at[3])
 
     send(r2, r3, device(dc=1), send_sem.at[8], recv_sem.at[8])
     half = NZ * 8
@@ -386,10 +396,6 @@
     for k in range(1, NX):
         at = pl.ds(pl.multiple_of(((x + k) % NX) * share, share), share)
         send(pbuf.at[at], precv.at[k - 1], device(dx=k), send_sem.at[9], recv_sem.at[9])
-    await_bytes(precv, recv_sem.at[9])
-    sfull[x] = sfull[x] + pbuf[my_share, :] + precv[0] + precv[1] + precv[2]
-    for k in range(1, NX):
-        send(sfull.at[x], sfull.at[x], device(dx=k), send_sem.at[16], recv_sem.at[16])
 
     await_bytes(rz, recv_sem.at[7])
     total = u[pl.ds(pl.multiple_of(z * JR, JR), JR), :]
@@ -399,6 +405,10 @@
     for k in range(1, NX):
         send(gfull.at[x], gfull.at[x], device(dx=k), send_sem.at[10], recv_sem.at[10])
 
+    await_bytes(precv, recv_sem.at[9])
+    sfull[x] = sfull[x] + pbuf[my_share, :] + precv[0] + precv[1] + precv[2]
+    for k in range(1, NX):
+        send(sfull.at[x], sfull.at[x], device(dx=k), send_sem.at[16], recv_sem.at[16])
     await_bytes(sfull.at[0:NX - 1], recv_sem.at[16])
     for q in range(NX):
         for k in range(3):
@@ -408,14 +418,18 @@
 
     await_bytes(csend, csend_sem)
     for ref, n in ((srecv, 0), (rx0, 1), (rx1, 2),
-                   (rl0.at[0], 11), (rl0.at[1], 12), (rl1.at[0], 13), (rl1.at[1], 14), (r1.at[0:NZ - 1], 3), (ry0, 4), (ry1, 5),
+                   (rl0.at[0], 11), (rl0.at[1], 12), (rl1.at[0], 13), (rl1.at[1], 14), (ry0, 4), (ry1, 5),
                    (rz, 7), (r3, 8), (precv, 9), (gfull.at[0:NX - 1], 10),
                    (state.at[0:NX - 1], 15), (sfull.at[0:NX - 1], 16)):
         await_bytes(ref, send_sem.at[n])
 
     @pl.when(partner_y != y)
     def _():
-        await_bytes(r1, send_sem.at[6])
+        await_bytes(r2, send_sem.at[3])
+
+    @pl.when(partner_y == y)
+    def _():
+        await_bytes(r2.at[0:NZ - 1], send_sem.at[3])
 
 
 def adamw_update(moment_one, moment_two, weight, gradient_rows):
@@ -467,7 +481,7 @@
             buf(2, chunk), buf(2, chunk), buf(chunk), buf(chunk),
             buf(NY - 1, piece), buf(NX - 1, piece), buf(2 * piece),
             buf(NZ - 1, JR), buf(NX, JR),
-            buf(NX - 1, 3 * JR), buf(NX, 3 * JR), buf(half_z), buf(NZ, 8), buf(NZ, 8), buf(NZ, 8),
+            buf(NX - 1, 3 * JR), buf(NX, 3 * JR), buf(half_z), buf(NZ, 8), buf(NZ, 8),
             buf(3 * blk), buf(NX - 1, 3 * JR), buf(NX, 3 * JR),
             dma, dma((6,)), dma, dma((2 * NX,)), dma((17,)), dma((17,)),
         ],

time: 49.1 us -> 49.5 us (level)
  the two profiles are of different devices: /device:TPU:1 before, /device:TPU:24 now
where the time goes in v6:
time: 49.5 us; the launch traced here: 49.1 us
  Pallas kernels  47.1 us (95%)
  other arithmetic  1.4 us (3%)
  between operations  0.64 us (1%)
    pallas_call x1, Pallas kernels, on_device(): pl.pallas_call(exchange, out_shape=jax.ShapeDtypeStruct((4 * blk, LANES),...  45.1 us
    pallas_call x1, Pallas kernels, on_device(): pl.pallas_call(prepare, grid=(1,), out_shape=[jax.ShapeDtypeStruct(table,...  1.98 us
    sub x1, other arithmetic, adamw_update(): return (first, second, weight - LEARN_RATE * (update + DECAY_RATE * weight))  1.4 us

profile of v6, /device:TPU:24, one launch (start us, length us, event | category | flops | bytes accessed | tf_op | source)
XLA Modules:
  0.0 49.1 jit_solution(4672279248006066391)
XLA Ops:
  0.6 2.0 %shard_map.103 = (s32[32,128]{1,0:T(8,128)}, f32[96,128]{1,0:T(8,128)}, f32[128,128]{1,0:T(8,128)}, f32[96,256]{1,0:T(8,128)}, f32[24,128]{1,0:T(8,128)}, /*index=5*/f32[24,128]{1,0:T(8,128)}) custom-call(s32[32,128]{1,0:T(8,128)} %bitcast.10, s32[32,128]{1,0:T(8,128)} %bitcast.11, s32[32,128]{1,0:T(8,128)} %bitcast.12, f32[32,128]{1,0:T(8,128)} %bitcast.13, ...), custom_call_target="tpu_custom_call" | custom-call | tf_op jit(solution)/shard_map/pallas_call | solution.py:461
  2.6 45.1 %shard_map.104 = f32[128,128]{1,0:T(8,128)} custom-call(s32[4096]{0:T(1024)} %bitcast.9, f32[96,128]{1,0:T(8,128)} %get-tuple-element.10.masked_hbm, f32[128,128]{1,0:T(8,128)} %get-tuple-element.11.wout_hbm, f32[96,256]{1,0:T(8,128)} %get-tuple-element.12.wsel_hbm, f32[24,128]{1,0:T(8,128)} %get-tuple-element.13.wstay_hbm, ...), custom_call_target="tpu_custom_call" | custom-call | flops 524288 | bytes 2097152 | tf_op jit(solution)/shard_map/pallas_call | solution.py:472
  47.7 1.4 %multiply_subtract_fusion = (f32[32,128]{1,0:T(8,128)}, f32[32,128]{1,0:T(8,128)}, f32[32,128]{1,0:T(8,128)}) fusion(f32[128,128]{1,0:T(8,128)} %shard_map.104), kind=kLoop, calls=%fused_computation.2 | loop fusion | flops 61440 | bytes 114688 | tf_op jit(solution)/shard_map/sub | solution.py:439

commit v7 on v6

--- a/solution.py
+++ b/solution.py
@@ -310,8 +310,8 @@
             send(own.at[high], landing.at[0, part:chunk], up, *straight)
         elif k == 3:
             send(own.at[low], landing.at[1, 0:part], down, *straight)
-        for earlier in {3: [2], 4: [3], 5: [4, 5]}.get(i, []):
-            pass_on(earlier)
+        if i >= 4:
+            pass_on(i - 2)
         if i == 2:
             await_bytes(srecv, recv_sem.at[0])
             state[x] = masked_ref[my_share, :] + srecv[0] + srecv[1] + srecv[2]
@@ -339,12 +339,10 @@
             def _():
                 r2[z] = ssum[pl.ds(pl.multiple_of(z * 8, 8), 8), :]
 
-    lag = 3
-    for i in range(len(chunks) + lag):
-        if i < len(chunks):
-            for_partner(i)
-        if i >= lag:
-            for_me(i - lag)
+    for i in range(len(chunks)):
+        for_partner(i)
+    for i in range(len(chunks)):
+        for_me(i)
 
     own0 = pl.multiple_of(x * chunk, chunk)
     own1 = pl.multiple_of((NX + y) * chunk, chunk)

time: 49.5 us -> 50.3 us (1.016)
  Pallas kernels: 47.1 us -> 47.9 us
    pallas_call x1, Pallas kernels: 45.1 us -> 45.9 us  [on_device(): pl.pallas_call(exchange, out_shape=jax.ShapeDtypeStruct((4 * blk, LANES),...]
where the time goes in v7:
time: 50.3 us; the launch traced here: 50 us
  Pallas kernels  47.9 us (95%)
  other arithmetic  1.4 us (3%)
  between operations  0.64 us (1%)
    pallas_call x1, Pallas kernels, on_device(): pl.pallas_call(exchange, out_shape=jax.ShapeDtypeStruct((4 * blk, LANES),...  45.9 us
    pallas_call x1, Pallas kernels, on_device(): pl.pallas_call(prepare, grid=(1,), out_shape=[jax.ShapeDtypeStruct(table,...  1.98 us
    sub x1, other arithmetic, adamw_update(): return (first, second, weight - LEARN_RATE * (update + DECAY_RATE * weight))  1.4 us

profile of v7, /device:TPU:24, one launch (start us, length us, event | category | flops | bytes accessed | tf_op | source)
XLA Modules:
  0.0 50.0 jit_solution(1584504032039458714)
XLA Ops:
  0.6 2.0 %shard_map.103 = (s32[32,128]{1,0:T(8,128)}, f32[96,128]{1,0:T(8,128)}, f32[128,128]{1,0:T(8,128)}, f32[96,256]{1,0:T(8,128)}, f32[24,128]{1,0:T(8,128)}, /*index=5*/f32[24,128]{1,0:T(8,128)}) custom-call(s32[32,128]{1,0:T(8,128)} %bitcast.10, s32[32,128]{1,0:T(8,128)} %bitcast.11, s32[32,128]{1,0:T(8,128)} %bitcast.12, f32[32,128]{1,0:T(8,128)} %bitcast.13, ...), custom_call_target="tpu_custom_call" | custom-call | tf_op jit(solution)/shard_map/pallas_call | solution.py:459
  2.6 45.9 %shard_map.104 = f32[128,128]{1,0:T(8,128)} custom-call(s32[4096]{0:T(1024)} %bitcast.9, f32[96,128]{1,0:T(8,128)} %get-tuple-element.10.masked_hbm, f32[128,128]{1,0:T(8,128)} %get-tuple-element.11.wout_hbm, f32[96,256]{1,0:T(8,128)} %get-tuple-element.12.wsel_hbm, f32[24,128]{1,0:T(8,128)} %get-tuple-element.13.wstay_hbm, ...), custom_call_target="tpu_custom_call" | custom-call | flops 524288 | bytes 2097152 | tf_op jit(solution)/shard_map/pallas_call | solution.py:470
  48.6 1.4 %multiply_subtract_fusion = (f32[32,128]{1,0:T(8,128)}, f32[32,128]{1,0:T(8,128)}, f32[32,128]{1,0:T(8,128)}) fusion(f32[128,128]{1,0:T(8,128)} %shard_map.104), kind=kLoop, calls=%fused_computation.2 | loop fusion | flops 61440 | bytes 114688 | tf_op jit(solution)/shard_map/sub | solution.py:437

commit v8 on v4

--- a/solution.py
+++ b/solution.py
@@ -176,7 +176,7 @@
 def exchange(order_hbm, out_hbm, wsel_hbm, stay_hbm, aux_hbm, grad_hbm, result_ref,
              order, out_ref, wsel_ref, stay_ref, aux_ref,
              grad, csend, crecv, own, rl0, rl1, rx0, rx1, t0, t1, ry0, ry1, u, rz, gfull,
-             srecv, ssum, r1, r2, r3, pbuf, precv,
+             srecv, ssum, r2, r3, pbuf, precv,
              grad_sem, in_sem, csend_sem, crecv_sem, send_sem, recv_sem):
     blk = NX * JR
     zh = NZ // 2
@@ -213,6 +213,16 @@
         return carry
 
     lax.fori_loop(1, NZ, greet, 0)
+    partner_y = (x - y + NX) % NX
+
+    @pl.when(partner_y != y)
+    def _():
+        def greet_far(to_z, carry):
+            pl.semaphore_signal(barrier, inc=1, device_id=((partner_y * NZ + to_z) * 2 + c, x),
+                                device_id_type=MESH)
+            return carry
+
+        lax.fori_loop(0, NZ, greet_far, 0)
 
     def send(src, dst, to, s_sem, r_sem):
         pltpu.make_async_remote_copy(
@@ -250,7 +260,8 @@
         base = chunks[i][2]
         gather(csend, base, (1 - c) * core_rows + base)
         if i == 0:
-            pl.semaphore_wait(barrier, len(peers) + NZ - 1)
+            pl.semaphore_wait(
+                barrier, len(peers) + NZ - 1 + jnp.where(partner_y != y, NZ, 0).astype(I32))
             for dx in range(1, NX):
                 to_y = (x + dx - y + NX) % NX
                 send(out_ref.at[pl.ds(pl.multiple_of(to_y * NZ * 8, NZ * 8), NZ * 8)],
@@ -260,7 +271,6 @@
 
     alive_mine = aux_ref[0:1, :]
     alive_other = aux_ref[8:9, :]
-    partner_y = (x - y + NX) % NX
     part = chunk // 2
     relays, landings = (rl0, rl1), (rx0, rx1)
 
@@ -295,21 +305,28 @@
             send(own.at[low], landing.at[1, 0:part], down, *straight)
         for earlier in {3: [2], 4: [3], 5: [4, 5]}.get(i, []):
             pass_on(earlier)
-        if i == 3:
+        if i == 5:
             await_bytes(srecv, recv_sem.at[0])
             total = out_ref[pl.ds(pl.multiple_of(partner_y * NZ * 8, NZ * 8), NZ * 8), :]
             for dx in range(NX - 1):
                 total = total + srecv[dx]
             ssum[...] = total
-            r1[z] = ssum[pl.ds(pl.multiple_of(z * 8, 8), 8), :]
 
             def spread(kz, carry):
                 to_z = (z + kz) % NZ
-                send(ssum.at[pl.ds(pl.multiple_of(to_z * 8, 8), 8)], r1.at[z],
-                     device(dz=kz), send_sem.at[3], recv_sem.at[3])
+                send(ssum.at[pl.ds(pl.multiple_of(to_z * 8, 8), 8)], r2.at[z],
+                     ((partner_y * NZ + to_z) * 2 + c, x), send_sem.at[3], recv_sem.at[3])
                 return carry
 
             lax.fori_loop(1, NZ, spread, 0)
+
+            @pl.when(partner_y != y)
+            def _():
+                spread(0, 0)
+
+            @pl.when(partner_y == y)
+            def _():
+                r2[z] = ssum[pl.ds(pl.multiple_of(z * 8, 8), 8), :]
 
     lag = 3
     for i in range(len(chunks) + lag):
@@ -331,17 +348,6 @@
         at = pl.ds(pl.multiple_of(((x + k) % NX) * piece, piece), piece)
         send(t1.at[at], ry1.at[k - 1], device(dx=k), send_sem.at[5], recv_sem.at[5])
 
-    await_bytes(r1.at[0:NZ - 1], recv_sem.at[3])
-    partner = ((partner_y * NZ + z) * 2 + c, x)
-
-    @pl.when(partner_y != y)
-    def _():
-        send(r1, r2, partner, send_sem.at[6], recv_sem.at[6])
-
-    @pl.when(partner_y == y)
-    def _():
-        r2[...] = r1[...]
-
     await_bytes(ry0, recv_sem.at[4])
     total = t0[pl.ds(pl.multiple_of(y * piece, piece), piece), :]
     for k in range(NY - 1):
@@ -363,7 +369,11 @@
 
     @pl.when(partner_y != y)
     def _():
-        await_bytes(r2, recv_sem.at[6])
+        await_bytes(r2, recv_sem.at[3])
+
+    @pl.when(partner_y == y)
+    def _():
+        await_bytes(r2.at[0:NZ - 1], recv_sem.at[3])
 
     send(r2, r3, device(dc=1), send_sem.at[8], recv_sem.at[8])
     half = NZ * 8
@@ -393,13 +403,17 @@
 
     await_bytes(csend, csend_sem)
     for ref, n in ((srecv, 0), (rx0, 1), (rx1, 2),
-                   (rl0.at[0], 11), (rl0.at[1], 12), (rl1.at[0], 13), (rl1.at[1], 14), (r1.at[0:NZ - 1], 3), (ry0, 4), (ry1, 5),
+                   (rl0.at[0], 11), (rl0.at[1], 12), (rl1.at[0], 13), (rl1.at[1], 14), (ry0, 4), (ry1, 5),
                    (rz, 7), (r3, 8), (precv, 9), (gfull.at[0:NX - 1], 10)):
         await_bytes(ref, send_sem.at[n])
 
     @pl.when(partner_y != y)
     def _():
-        await_bytes(r1, send_sem.at[6])
+        await_bytes(r2, send_sem.at[3])
+
+    @pl.when(partner_y == y)
+    def _():
+        await_bytes(r2.at[0:NZ - 1], send_sem.at[3])
 
 
 def adamw_update(moment_one, moment_two, weight, gradient_rows):
@@ -452,7 +466,7 @@
             buf(2, chunk), buf(2, chunk), buf(chunk), buf(chunk),
             buf(NY - 1, piece), buf(NX - 1, piece), buf(2 * piece),
             buf(NZ - 1, JR), buf(NX, JR),
-            buf(NX - 1, half_z), buf(half_z), buf(NZ, 8), buf(NZ, 8), buf(NZ, 8),
+            buf(NX - 1, half_z), buf(half_z), buf(NZ, 8), buf(NZ, 8),
             buf(3 * blk), buf(NX - 1, 3 * blk),
             dma, dma((5,)), dma, dma((2 * NX,)), dma((15,)), dma((15,)),
         ],

time: 48.8 us -> 50.6 us (1.037)
  the two profiles are of different devices: /device:TPU:2 before, /device:TPU:24 now
where the time goes in v8:
time: 50.6 us; the launch traced here: 50.2 us
  Pallas kernels  48.2 us (95%)
  other arithmetic  1.4 us (3%)
  between operations  0.64 us (1%)
    pallas_call x1, Pallas kernels, on_device(): pl.pallas_call(exchange, out_shape=jax.ShapeDtypeStruct((4 * blk, LANES),...  45.6 us
    pallas_call x1, Pallas kernels, on_device(): pl.pallas_call(prepare, grid=(1,), out_shape=[jax.ShapeDtypeStruct(table,...  2.56 us
    sub x1, other arithmetic, adamw_update(): return (first, second, weight - LEARN_RATE * (update + DECAY_RATE * weight))  1.4 us

profile of v8, /device:TPU:24, one launch (start us, length us, event | category | flops | bytes accessed | tf_op | source)
XLA Modules:
  0.0 50.2 jit_solution(2420819183542815069)
XLA Ops:
  0.6 2.6 %shard_map.103 = (s32[32,128]{1,0:T(8,128)}, f32[512,128]{1,0:T(8,128)}, f32[96,256]{1,0:T(8,128)}, f32[96,128]{1,0:T(8,128)}, f32[24,128]{1,0:T(8,128)}) custom-call(s32[32,128]{1,0:T(8,128)} %bitcast.10, s32[32,128]{1,0:T(8,128)} %bitcast.11, s32[32,128]{1,0:T(8,128)} %bitcast.12, f32[32,128]{1,0:T(8,128)} %bitcast.13, f32[32,128]{1,0:T(8,128)} %bitcast.14, ...), custom_call_target="tpu_custom_call" | custom-call | tf_op jit(solution)/shard_map/pallas_call | solution.py:445
  3.2 45.6 %shard_map.104 = f32[128,128]{1,0:T(8,128)} custom-call(s32[4096]{0:T(1024)} %bitcast.9, f32[512,128]{1,0:T(8,128)} %get-tuple-element.9.out_hbm, f32[96,256]{1,0:T(8,128)} %get-tuple-element.10.wsel_hbm, f32[96,128]{1,0:T(8,128)} %get-tuple-element.11.stay_hbm, f32[24,128]{1,0:T(8,128)} %get-tuple-element.12.aux_hbm, f32[4096,128]{1,0:T(8,128)} %bitcast.8), custom_call_target="tpu_custom_call" | custom-call | flops 524288 | bytes 2097152 | tf_op jit(solution)/shard_map/pallas_call | solution.py:457
  48.8 1.4 %multiply_subtract_fusion = (f32[32,128]{1,0:T(8,128)}, f32[32,128]{1,0:T(8,128)}, f32[32,128]{1,0:T(8,128)}) fusion(f32[128,128]{1,0:T(8,128)} %shard_map.104), kind=kLoop, calls=%fused_computation.2 | loop fusion | flops 61440 | bytes 114688 | tf_op jit(solution)/shard_map/sub | solution.py:423

commit v9 on v3

--- a/solution.py
+++ b/solution.py
@@ -292,7 +292,7 @@
             send(own.at[low], landing.at[1, 0:part], down, *straight)
         if i >= 4:
             pass_on(i - 2)
-        if i == len(chunks) // 2:
+        if i == 1:
             await_bytes(srecv, recv_sem.at[0])
             total = out_ref[pl.ds(pl.multiple_of(partner_y * NZ * 8, NZ * 8), NZ * 8), :]
             for dx in range(NX - 1):

time: 47.9 us -> 47.8 us (level)
  no operation moved by 1% of the time
where the time goes in v9:
time: 47.8 us; the launch traced here: 47.4 us
  Pallas kernels  45.4 us (95%)
  other arithmetic  1.4 us (3%)
  between operations  0.64 us (1%)
    pallas_call x1, Pallas kernels, on_device(): pl.pallas_call(exchange, out_shape=jax.ShapeDtypeStruct((4 * blk, LANES),...  42.8 us
    pallas_call x1, Pallas kernels, on_device(): pl.pallas_call(prepare, grid=(1,), out_shape=[jax.ShapeDtypeStruct(table,...  2.56 us
    sub x1, other arithmetic, adamw_update(): return (first, second, weight - LEARN_RATE * (update + DECAY_RATE * weight))  1.4 us

profile of v9, /device:TPU:8, one launch (start us, length us, event | category | flops | bytes accessed | tf_op | source)
XLA Modules:
  0.0 47.4 jit_solution(3386466309551449735)
XLA Ops:
  0.6 2.6 %shard_map.103 = (s32[32,128]{1,0:T(8,128)}, f32[512,128]{1,0:T(8,128)}, f32[96,256]{1,0:T(8,128)}, f32[96,128]{1,0:T(8,128)}, f32[24,128]{1,0:T(8,128)}) custom-call(s32[32,128]{1,0:T(8,128)} %bitcast.10, s32[32,128]{1,0:T(8,128)} %bitcast.11, s32[32,128]{1,0:T(8,128)} %bitcast.12, f32[32,128]{1,0:T(8,128)} %bitcast.13, f32[32,128]{1,0:T(8,128)} %bitcast.14, ...), custom_call_target="tpu_custom_call" | custom-call | tf_op jit(solution)/shard_map/pallas_call | solution.py:421
  3.2 42.8 %shard_map.104 = f32[128,128]{1,0:T(8,128)} custom-call(s32[4096]{0:T(1024)} %bitcast.9, f32[512,128]{1,0:T(8,128)} %get-tuple-element.9.out_hbm, f32[96,256]{1,0:T(8,128)} %get-tuple-element.10.wsel_hbm, f32[96,128]{1,0:T(8,128)} %get-tuple-element.11.stay_hbm, f32[24,128]{1,0:T(8,128)} %get-tuple-element.12.aux_hbm, f32[4096,128]{1,0:T(8,128)} %bitcast.8), custom_call_target="tpu_custom_call" | custom-call | flops 524288 | bytes 2097152 | tf_op jit(solution)/shard_map/pallas_call | solution.py:433
  46.0 1.4 %multiply_subtract_fusion = (f32[32,128]{1,0:T(8,128)}, f32[32,128]{1,0:T(8,128)}, f32[32,128]{1,0:T(8,128)}) fusion(f32[128,128]{1,0:T(8,128)} %shard_map.104), kind=kLoop, calls=%fused_computation.2 | loop fusion | flops 61440 | bytes 114688 | tf_op jit(solution)/shard_map/sub | solution.py:399

commit v10 on v9

--- a/solution.py
+++ b/solution.py
@@ -308,6 +308,17 @@
 
             lax.fori_loop(1, NZ, spread, 0)
 
+    await_bytes(r1.at[0:NZ - 1], recv_sem.at[3])
+    partner = ((partner_y * NZ + z) * 2 + c, x)
+
+    @pl.when(partner_y != y)
+    def _():
+        send(r1, r2, partner, send_sem.at[6], recv_sem.at[6])
+
+    @pl.when(partner_y == y)
+    def _():
+        r2[...] = r1[...]
+
     own0 = pl.multiple_of(x * chunk, chunk)
     own1 = pl.multiple_of((NX + y) * chunk, chunk)
     await_bytes(rx0, recv_sem.at[1])
@@ -320,17 +331,6 @@
     for k in range(1, NX):
         at = pl.ds(pl.multiple_of(((x + k) % NX) * piece, piece), piece)
         send(t1.at[at], ry1.at[k - 1], device(dx=k), send_sem.at[5], recv_sem.at[5])
-
-    await_bytes(r1.at[0:NZ - 1], recv_sem.at[3])
-    partner = ((partner_y * NZ + z) * 2 + c, x)
-
-    @pl.when(partner_y != y)
-    def _():
-        send(r1, r2, partner, send_sem.at[6], recv_sem.at[6])
-
-    @pl.when(partner_y == y)
-    def _():
-        r2[...] = r1[...]
 
     await_bytes(ry0, recv_sem.at[4])
     total = t0[pl.ds(pl.multiple_of(y * piece, piece), piece), :]

time: 47.8 us -> 52 us (1.088)
  the two profiles are of different devices: /device:TPU:8 before, /device:TPU:24 now
where the time goes in v10:
time: 52 us; the launch traced here: 51.5 us
  Pallas kernels  49.4 us (95%)
  other arithmetic  1.4 us (3%)
  between operations  0.64 us (1%)
    pallas_call x1, Pallas kernels, on_device(): pl.pallas_call(exchange, out_shape=jax.ShapeDtypeStruct((4 * blk, LANES),...  46.9 us
    pallas_call x1, Pallas kernels, on_device(): pl.pallas_call(prepare, grid=(1,), out_shape=[jax.ShapeDtypeStruct(table,...  2.56 us
    sub x1, other arithmetic, adamw_update(): return (first, second, weight - LEARN_RATE * (update + DECAY_RATE * weight))  1.4 us

profile of v10, /device:TPU:24, one launch (start us, length us, event | category | flops | bytes accessed | tf_op | source)
XLA Modules:
  0.0 51.5 jit_solution(11389483274972267745)
XLA Ops:
  0.6 2.6 %shard_map.103 = (s32[32,128]{1,0:T(8,128)}, f32[512,128]{1,0:T(8,128)}, f32[96,256]{1,0:T(8,128)}, f32[96,128]{1,0:T(8,128)}, f32[24,128]{1,0:T(8,128)}) custom-call(s32[32,128]{1,0:T(8,128)} %bitcast.10, s32[32,128]{1,0:T(8,128)} %bitcast.11, s32[32,128]{1,0:T(8,128)} %bitcast.12, f32[32,128]{1,0:T(8,128)} %bitcast.13, f32[32,128]{1,0:T(8,128)} %bitcast.14, ...), custom_call_target="tpu_custom_call" | custom-call | tf_op jit(solution)/shard_map/pallas_call | solution.py:421
  3.2 46.9 %shard_map.104 = f32[128,128]{1,0:T(8,128)} custom-call(s32[4096]{0:T(1024)} %bitcast.9, f32[512,128]{1,0:T(8,128)} %get-tuple-element.9.out_hbm, f32[96,256]{1,0:T(8,128)} %get-tuple-element.10.wsel_hbm, f32[96,128]{1,0:T(8,128)} %get-tuple-element.11.stay_hbm, f32[24,128]{1,0:T(8,128)} %get-tuple-element.12.aux_hbm, f32[4096,128]{1,0:T(8,128)} %bitcast.8), custom_call_target="tpu_custom_call" | custom-call | flops 524288 | bytes 2097152 | tf_op jit(solution)/shard_map/pallas_call | solution.py:433
  50.1 1.4 %multiply_subtract_fusion = (f32[32,128]{1,0:T(8,128)}, f32[32,128]{1,0:T(8,128)}, f32[32,128]{1,0:T(8,128)}) fusion(f32[128,128]{1,0:T(8,128)} %shard_map.104), kind=kLoop, calls=%fused_computation.2 | loop fusion | flops 61440 | bytes 114688 | tf_op jit(solution)/shard_map/sub | solution.py:399
